TPU v7x, 32 devices: a whole 2x2x4 slice. The times are simulated.
32 devices in a mesh: row: 4 (over z), blk: 8 (over y, x, core).
Axes of the slice: x: 2, y: 2, z: 4, core: 2. Of those that a mesh axis runs over, the one named last changes fastest.
Arguments:
- tokens: bfloat16 [16, 1024, 768], P('row', 'blk'), may hold values from -6 to 6
- lengths: int32 [16, 8], P('row'), may hold values from 20 to 884, as said below
- norm_gain: bfloat16 [768], P('blk'), may hold values from 0.5 to 1.5
- qkv_weight: bfloat16 [768, 2304], P('blk', 'row'), may hold values from -0.21875 to 0.21875
- out_weight: bfloat16 [768, 768], P('blk', 'row'), may hold values from -6 to 6
- mlp_gain: bfloat16 [768], P('blk'), may hold values from 0.5 to 1.5
- in_weight: bfloat16 [768, 2304], P('blk', 'row'), may hold values from -0.21875 to 0.21875
- down_weight: bfloat16 [1152, 768], P('blk', 'row'), may hold values from -0.1875 to 0.1875
- cotangent: bfloat16 [16, 1024, 768], P('row', 'blk'), may hold values from -6 to 6
Outputs:
- output: bfloat16 [16, 1024, 768], P('row', 'blk')
- input_grad: bfloat16 [16, 1024, 768], P('row', 'blk')
- norm_gain_grad: float32 [768], P('blk')
- qkv_grad: float32 [768, 2304], P('blk', 'row')
- out_grad: float32 [768, 768], P('blk', 'row')
- mlp_gain_grad: float32 [768], P('blk')
- in_grad: float32 [768, 2304], P('blk', 'row')
- down_grad: float32 [1152, 768], P('blk', 'row')
Inputs may be any that keep to these rules, and one draw needn't show every extreme that they name: Each packed row holds 8 positive document lengths that sum to 1024.
All inputs are finite; a program needn't handle non-finite values.
Results may differ from a plain program's by a relative error of at most 0.03.
Values may be sent and summed in bfloat16 or wider, within the bound.
No kernel may reach another device: no remote copies, remote signals or barrier semaphores. Data moves between devices by JAX's collectives and lax.ppermute only.
A program may use at most 256 MiB of HBM per device.

v0:
```python
import math

import jax
import jax.numpy as jnp
from jax import lax
from jax.sharding import PartitionSpec as P

D = 768
HEADS = 12
HD = 64
FF = 1152


ROPE_BASE = 160000.0
NORM_EPSILON = 1e-05
MASKED = -1e30


def layer_norm(values, gain_vec):
    average = jnp.mean(values, axis=-1, keepdims=True)
    centred = values - average
    inv_std = lax.rsqrt(jnp.mean(centred * centred, axis=-1, keepdims=True) + NORM_EPSILON)
    normalized = centred * inv_std
    return (normalized * gain_vec, normalized, inv_std)


def norm_backward(grad_out, normalized, inv_std, gain_vec):
    gain_grad = jnp.sum(grad_out * normalized, axis=(0, 1))
    scaled = grad_out * gain_vec
    inner = jnp.mean(scaled * normalized, axis=-1, keepdims=True)
    return (
        gain_grad,
        inv_std * (scaled - jnp.mean(scaled, axis=-1, keepdims=True) - normalized * inner),
    )


def doc_tables(lengths, first_tok, tok_count):
    doc_ends = jnp.cumsum(lengths, axis=-1)
    places = first_tok + jnp.arange(tok_count, dtype=jnp.int32)
    passed = places[None, :, None] >= doc_ends[:, None, :]
    docs = jnp.sum(passed.astype(jnp.int32), axis=2)
    starts = jnp.sum(jnp.where(passed, lengths[:, None, :], 0), axis=2)
    return (docs, places[None, :] - starts)


def rotate(values, positions, direction):
    half_dim = HD // 2
    inverse = ROPE_BASE ** (-(jnp.arange(half_dim, dtype=jnp.float32) * (2.0 / HD)))
    angles = positions.astype(jnp.float32)[..., None] * inverse
    cosine = jnp.cos(angles)[..., None, :]
    sine_part = direction * jnp.sin(angles)[..., None, :]
    front_half = values[..., :half_dim]
    back_half = values[..., half_dim:]
    return jnp.concatenate(
        [front_half * cosine - back_half * sine_part, back_half * cosine + front_half * sine_part],
        axis=-1,
    )


def row_intersections(query_docs, key_docs):
    return (query_docs[0] <= key_docs[-1]) & (key_docs[0] <= query_docs[-1])


def by_blocks(running, total_rows, take, update):
    block_size = math.gcd(total_rows, 512)

    def one_block(block_index, state):
        offset = block_index * block_size
        return update(state, take(offset, block_size), offset, block_size)

    return lax.fori_loop(0, total_rows // block_size, one_block, running)


def unchanged(state):
    return state


def body(
    tokens, lengths, norm_gain, qkv_weight, out_weight, mlp_gain, in_weight, down_weight, cotangent
):
    row_count, tok_count, _ = tokens.shape
    scale_factor = 1.0 / math.sqrt(HD)
    first_tok = lax.axis_index("blk") * tok_count
    heads_shape = (row_count, tok_count, HEADS, HD)
    flat_shape = (row_count, tok_count, D)
    w_qkv, w_out, w_in, w_down = (
        lax.all_gather(qkv_weight, "row", axis=1, tiled=True),
        lax.all_gather(out_weight, "row", axis=1, tiled=True),
        lax.all_gather(in_weight, "row", axis=1, tiled=True),
        lax.all_gather(down_weight, "row", axis=1, tiled=True),
    )
    w_qkv, w_out, w_in, w_down, gain_one, gain_two = (
        lax.all_gather(w_qkv, "blk", axis=0, tiled=True),
        lax.all_gather(w_out, "blk", axis=0, tiled=True),
        lax.all_gather(w_in, "blk", axis=0, tiled=True),
        lax.all_gather(w_down, "blk", axis=0, tiled=True),
        lax.all_gather(norm_gain, "blk", axis=0, tiled=True),
        lax.all_gather(mlp_gain, "blk", axis=0, tiled=True),
    )
    gain_one = gain_one.astype(jnp.float32)
    gain_two = gain_two.astype(jnp.float32)
    query_docs, query_pos = doc_tables(lengths, first_tok, tok_count)
    inputs = tokens.astype(jnp.float32)
    normed_one, unit_one, inv_one = layer_norm(inputs, gain_one)
    normed_low = normed_one.astype(jnp.bfloat16)
    projected = jnp.einsum("rtd,de->rte", normed_low, w_qkv, preferred_element_type=jnp.float32)
    queries = rotate(projected[..., :D].reshape(heads_shape), query_pos, 1.0).astype(jnp.bfloat16)
    keys = rotate(projected[..., D : 2 * D].reshape(heads_shape), query_pos, 1.0).astype(
        jnp.bfloat16
    )
    values = projected[..., 2 * D :].reshape(heads_shape).astype(jnp.bfloat16)

    def sent_keys(pieces):

        def take(offset, block_size):
            block_shape = (row_count, block_size, HEADS, HD)
            return tuple(
                (
                    lax.dynamic_slice_in_dim(member, offset, block_size, 1).reshape(block_shape)
                    for member in pieces
                )
            )

        return take

    def attend(state, block, key_first, block_size):
        key_docs, _ = doc_tables(lengths, key_first, block_size)
        block_keys, block_values = block

        def attend_per_row(item):
            running, row_queries, row_qdocs, row_keys, row_values, row_kdocs = item

            def attend_accumulate(current):
                top_score, row_total, weighted = current
                scores = (
                    jnp.einsum(
                        "qhd,khd->hqk", row_queries, row_keys, preferred_element_type=jnp.float32
                    )
                    * scale_factor
                )
                same_doc = row_qdocs[None, :, None] == row_kdocs[None, None, :]
                scores = jnp.where(same_doc, scores, MASKED)
                new_top = jnp.maximum(top_score, jnp.max(scores, axis=-1))
                rescale = jnp.exp(top_score - new_top)
                probs = jnp.exp(scores - new_top[..., None])
                row_total = row_total * rescale + jnp.sum(probs, axis=-1)
                weighted = weighted * rescale[..., None] + jnp.einsum(
                    "hqk,khd->hqd",
                    probs.astype(jnp.bfloat16),
                    row_values,
                    preferred_element_type=jnp.float32,
                )
                return (new_top, row_total, weighted)

            return lax.cond(
                row_intersections(row_qdocs, row_kdocs), attend_accumulate, unchanged, running
            )

        return lax.map(
            attend_per_row, (state, queries, query_docs, block_keys, block_values, key_docs)
        )

    start_state = (
        jnp.full((row_count, HEADS, tok_count), MASKED, jnp.float32),
        jnp.zeros((row_count, HEADS, tok_count), jnp.float32),
        jnp.zeros((row_count, HEADS, tok_count, HD), jnp.float32),
    )
    pieces = (
        lax.all_gather(keys.reshape(flat_shape), "blk", axis=1, tiled=True),
        lax.all_gather(values.reshape(flat_shape), "blk", axis=1, tiled=True),
    )
    top_score, row_total, weighted = by_blocks(
        start_state, pieces[0].shape[1], sent_keys(pieces), attend
    )
    log_total = top_score + jnp.log(row_total)
    attn_heads = weighted / row_total[..., None]
    attn_low = jnp.swapaxes(attn_heads, 1, 2).reshape(flat_shape).astype(jnp.bfloat16)
    hidden = inputs + jnp.einsum("rtd,de->rte", attn_low, w_out, preferred_element_type=jnp.float32)
    normed_two, unit_two, inv_two = layer_norm(hidden, gain_two)
    normed_two_low = normed_two.astype(jnp.bfloat16)
    gate_up = jnp.einsum("rtd,de->rte", normed_two_low, w_in, preferred_element_type=jnp.float32)
    gate_part = gate_up[..., :FF]
    up_part = gate_up[..., FF:]
    activated, gelu_pull = jax.vjp(lambda value: jax.nn.gelu(value, approximate=False), gate_part)
    middle = (activated * up_part).astype(jnp.bfloat16)
    output = (
        hidden + jnp.einsum("rtf,fd->rtd", middle, w_down, preferred_element_type=jnp.float32)
    ).astype(jnp.bfloat16)
    grad_down = jnp.einsum("rtf,rtd->fd", middle, cotangent, preferred_element_type=jnp.float32)
    grad_middle = jnp.einsum("rtd,fd->rtf", cotangent, w_down, preferred_element_type=jnp.float32)
    grad_gate = gelu_pull(grad_middle * up_part)[0]
    grad_up = grad_middle * activated
    grad_gate_up = jnp.concatenate([grad_gate, grad_up], axis=-1).astype(jnp.bfloat16)
    grad_in = jnp.einsum(
        "rtd,rte->de", normed_two_low, grad_gate_up, preferred_element_type=jnp.float32
    )
    grad_normed_two = jnp.einsum(
        "rte,de->rtd", grad_gate_up, w_in, preferred_element_type=jnp.float32
    )
    gain_two_part, grad_hidden_norm = norm_backward(grad_normed_two, unit_two, inv_two, gain_two)
    grad_hidden = cotangent.astype(jnp.float32) + grad_hidden_norm
    grad_branch = grad_hidden.astype(jnp.bfloat16)
    grad_out = jnp.einsum("rtd,rte->de", attn_low, grad_branch, preferred_element_type=jnp.float32)
    dout_low = jnp.einsum(
        "rte,de->rtd", grad_branch, w_out, preferred_element_type=jnp.float32
    ).astype(jnp.bfloat16)
    dout_heads = dout_low.reshape(heads_shape)
    delta = jnp.sum(jnp.swapaxes(dout_heads.astype(jnp.float32), 1, 2) * attn_heads, axis=-1)
    lse_all, delta_all = (
        lax.all_gather(log_total.astype(jnp.bfloat16), "blk", axis=2, tiled=True).astype(
            log_total.dtype
        ),
        lax.all_gather(delta.astype(jnp.bfloat16), "blk", axis=2, tiled=True).astype(delta.dtype),
    )

    def key_grads(state, block, query_first, block_size):
        block_queries, block_dout, block_lse, block_delta = block
        block_docs, _ = doc_tables(lengths, query_first, block_size)

        def key_per_row(item):
            (
                running,
                row_bq,
                row_bdout,
                row_blse,
                row_bdelta,
                row_bdocs,
                row_keys,
                row_values,
                row_kdocs,
            ) = item

            def key_accumulate(current):
                grad_keys, grad_values = current
                scores = (
                    jnp.einsum("qhd,khd->hqk", row_bq, row_keys, preferred_element_type=jnp.float32)
                    * scale_factor
                )
                same_doc = row_bdocs[None, :, None] == row_kdocs[None, None, :]
                probs = jnp.exp(jnp.where(same_doc, scores, MASKED) - row_blse[..., None])
                dprobs = jnp.einsum(
                    "qhd,khd->hqk", row_bdout, row_values, preferred_element_type=jnp.float32
                )
                dscores = (probs * (dprobs - row_bdelta[..., None])).astype(jnp.bfloat16)
                grad_values = grad_values + jnp.einsum(
                    "hqk,qhd->khd",
                    probs.astype(jnp.bfloat16),
                    row_bdout,
                    preferred_element_type=jnp.float32,
                )
                grad_keys = (
                    grad_keys
                    + jnp.einsum(
                        "hqk,qhd->khd", dscores, row_bq, preferred_element_type=jnp.float32
                    )
                    * scale_factor
                )
                return (grad_keys, grad_values)

            return lax.cond(
                row_intersections(row_bdocs, row_kdocs), key_accumulate, unchanged, running
            )

        return lax.map(
            key_per_row,
            (
                state,
                block_queries,
                block_dout,
                block_lse,
                block_delta,
                block_docs,
                keys,
                values,
                query_docs,
            ),
        )

    zero_heads = jnp.zeros(heads_shape, jnp.float32)
    pieces = (
        lax.all_gather(queries.reshape(flat_shape), "blk", axis=1, tiled=True),
        lax.all_gather(dout_low, "blk", axis=1, tiled=True),
    )

    def take(offset, block_size):
        block_shape = (row_count, block_size, HEADS, HD)
        query_part = lax.dynamic_slice_in_dim(pieces[0], offset, block_size, 1).reshape(block_shape)
        dout_part = lax.dynamic_slice_in_dim(pieces[1], offset, block_size, 1).reshape(block_shape)
        lse_part = lax.dynamic_slice_in_dim(lse_all, offset, block_size, 2)
        delta_part = lax.dynamic_slice_in_dim(delta_all, offset, block_size, 2)
        return (query_part, dout_part, lse_part, delta_part)

    grad_keys, grad_values = by_blocks(
        (zero_heads, zero_heads), pieces[0].shape[1], take, key_grads
    )

    def query_grads(state, block, key_first, block_size):
        key_docs, _ = doc_tables(lengths, key_first, block_size)
        block_keys, block_values = block

        def query_per_row(item):
            (
                running,
                row_queries,
                row_qdocs,
                row_lse,
                row_delta,
                row_dout,
                row_keys,
                row_values,
                row_kdocs,
            ) = item

            def query_accumulate(grad_queries):
                scores = (
                    jnp.einsum(
                        "qhd,khd->hqk", row_queries, row_keys, preferred_element_type=jnp.float32
                    )
                    * scale_factor
                )
                same_doc = row_qdocs[None, :, None] == row_kdocs[None, None, :]
                probs = jnp.exp(jnp.where(same_doc, scores, MASKED) - row_lse[..., None])
                dprobs = jnp.einsum(
                    "qhd,khd->hqk", row_dout, row_values, preferred_element_type=jnp.float32
                )
                dscores = (probs * (dprobs - row_delta[..., None])).astype(jnp.bfloat16)
                return (
                    grad_queries
                    + jnp.einsum(
                        "hqk,khd->qhd", dscores, row_keys, preferred_element_type=jnp.float32
                    )
                    * scale_factor
                )

            return lax.cond(
                row_intersections(row_qdocs, row_kdocs), query_accumulate, unchanged, running
            )

        return lax.map(
            query_per_row,
            (
                state,
                queries,
                query_docs,
                log_total,
                delta,
                dout_heads,
                block_keys,
                block_values,
                key_docs,
            ),
        )

    fold_pieces = (
        lax.all_gather(keys.reshape(flat_shape), "blk", axis=1, tiled=True),
        lax.all_gather(values.reshape(flat_shape), "blk", axis=1, tiled=True),
    )
    grad_queries = by_blocks(
        zero_heads, fold_pieces[0].shape[1], sent_keys(fold_pieces), query_grads
    )
    grad_projected = jnp.concatenate(
        [rotate(grad_queries, query_pos, -1.0), rotate(grad_keys, query_pos, -1.0), grad_values],
        axis=2,
    )
    grad_projected = grad_projected.reshape(row_count, tok_count, 3 * D).astype(jnp.bfloat16)
    grad_qkv = jnp.einsum(
        "rtd,rte->de", normed_low, grad_projected, preferred_element_type=jnp.float32
    )
    grad_normed_one = jnp.einsum(
        "rte,de->rtd", grad_projected, w_qkv, preferred_element_type=jnp.float32
    )
    gain_one_part, grad_input_norm = norm_backward(grad_normed_one, unit_one, inv_one, gain_one)
    input_grad = (grad_hidden + grad_input_norm).astype(jnp.bfloat16)
    sum_qkv, sum_out, sum_in, sum_down, sum_one, sum_two = (
        lax.psum_scatter(
            grad_qkv.astype(jnp.bfloat16), "blk", scatter_dimension=0, tiled=True
        ).astype(jnp.float32),
        lax.psum_scatter(
            grad_out.astype(jnp.bfloat16), "blk", scatter_dimension=0, tiled=True
        ).astype(jnp.float32),
        lax.psum_scatter(
            grad_in.astype(jnp.bfloat16), "blk", scatter_dimension=0, tiled=True
        ).astype(jnp.float32),
        lax.psum_scatter(
            grad_down.astype(jnp.bfloat16), "blk", scatter_dimension=0, tiled=True
        ).astype(jnp.float32),
        lax.psum_scatter(
            gain_one_part.astype(jnp.bfloat16), "blk", scatter_dimension=0, tiled=True
        ).astype(jnp.float32),
        lax.psum_scatter(
            gain_two_part.astype(jnp.bfloat16), "blk", scatter_dimension=0, tiled=True
        ).astype(jnp.float32),
    )
    sum_qkv, sum_out, sum_in, sum_down = (
        lax.psum_scatter(
            sum_qkv.astype(jnp.bfloat16), "row", scatter_dimension=1, tiled=True
        ).astype(jnp.float32),
        lax.psum_scatter(
            sum_out.astype(jnp.bfloat16), "row", scatter_dimension=1, tiled=True
        ).astype(jnp.float32),
        lax.psum_scatter(
            sum_in.astype(jnp.bfloat16), "row", scatter_dimension=1, tiled=True
        ).astype(jnp.float32),
        lax.psum_scatter(
            sum_down.astype(jnp.bfloat16), "row", scatter_dimension=1, tiled=True
        ).astype(jnp.float32),
    )
    sum_one, sum_two = lax.psum((sum_one, sum_two), "row")
    return (output, input_grad, sum_one, sum_qkv, sum_out, sum_two, sum_in, sum_down)


def solution(mesh):
    placed = (
        P("row", "blk", None),
        P("row", None),
        P("blk"),
        P("blk", "row"),
        P("blk", "row"),
        P("blk"),
        P("blk", "row"),
        P("blk", "row"),
        P("row", "blk", None),
    )
    return jax.shard_map(
        body,
        mesh=mesh,
        in_specs=placed,
        out_specs=(
            P("row", "blk", None),
            P("row", "blk", None),
            P("blk"),
            P("blk", "row"),
            P("blk", "row"),
            P("blk"),
            P("blk", "row"),
            P("blk", "row"),
        ),
        check_vma=False,
    )
```

profile of v0, /device:TPU:0, one launch (start us, length us, event | category | flops | bytes accessed | tf_op | source)
XLA Modules:
  0.0 875.4 jit_solution(9300875972767213462)
XLA Ops:
  7.3 17.3 %all-gather = bf16[4,576,96]{1,2,0:T(8,128)(2,1)S(1)} all-gather(bf16[1,576,96]{1,2,0:T(8,128)(2,1)} %bitcast.278), channel_id=1, replica_groups=mesh['row'=4,'blk'=8] {'row'}, dimensions={0}, use_global_device_ids=true | all-gather | bytes 552960 | tf_op jit(solution)/shard_map/all_gather | solution.py:87
  27.8 11.9 %all-reduce.6 = (bf16[768]{0:T(1024)(128)(2,1)S(1)}, bf16[768]{0:T(1024)(128)(2,1)S(1)}) all-reduce(bf16[768]{0:T(1024)(128)(2,1)S(1)} %dynamic-update-slice, bf16[768]{0:T(1024)(128)(2,1)S(1)} %dynamic-update-slice.1), channel_id=1, replica_groups=mesh['row'=4,'blk'=8] {'blk'}, use_global_device_ids=true, to_apply=%add | all-reduce | flops 1536 | bytes 6144
  40.4 21.6 %all-gather.12.cloned.1.call-done = bf16[768,2304]{1,0:T(8,128)(2,1)} async-done(((bf16[96,2304]{1,0:T(8,128)(2,1)}), bf16[768,2304]{1,0:T(8,128)(2,1)}) %all-gather.12.cloned.1.call-update) | async-done | bytes 3538960 | tf_op jit(solution)/shard_map/all_gather | solution.py:93
  81.5 13.7 %all_gather.55 = bf16[96,768]{0,1:T(8,128)(2,1)S(1)} all-gather(bf16[96,192]{0,1:T(8,128)(2,1)S(1)} %copy.76), channel_id=1, replica_groups=mesh['row'=4,'blk'=8] {'row'}, dimensions={1}, use_global_device_ids=true | all-gather | bytes 184320 | tf_op jit(solution)/shard_map/all_gather | solution.py:88
  96.0 16.1 %all-gather.1 = bf16[4,576,96]{1,2,0:T(8,128)(2,1)S(1)} all-gather(bf16[1,576,96]{1,2,0:T(8,128)(2,1)S(1)} %bitcast.279), channel_id=1, replica_groups=mesh['row'=4,'blk'=8] {'row'}, dimensions={0}, use_global_device_ids=true | all-gather | bytes 552960 | tf_op jit(solution)/shard_map/all_gather | solution.py:89
  113.7 14.1 %all-gather.2 = bf16[4,192,144]{1,2,0:T(8,128)(2,1)S(1)} all-gather(bf16[1,192,144]{1,2,0:T(8,128)(2,1)S(1)} %bitcast.281), channel_id=1, replica_groups=mesh['row'=4,'blk'=8] {'row'}, dimensions={0}, use_global_device_ids=true | all-gather | bytes 276480 | tf_op jit(solution)/shard_map/all_gather | solution.py:90
  130.7 8.7 copy.75
  139.4 24.7 %all-gather.14.cloned.1.call-done = bf16[4,1024,768]{1,2,0:T(8,128)(2,1)} async-done(((bf16[4,128,768]{1,2,0:T(8,128)(2,1)}), bf16[4,1024,768]{1,2,0:T(8,128)(2,1)}) %all-gather.14.cloned.1.call-update) | async-done | bytes 6291472 | tf_op jit(solution)/shard_map/all_gather | solution.py:169
  166.7 155.0 %while.139 = (s32[]{:T(128)}, f32[4,12,128]{2,1,0:T(8,128)}, f32[4,12,128]{2,1,0:T(8,128)}, f32[4,12,128,64]{2,3,1,0:T(8,128)}, bf16[4,1024,768]{1,2,0:T(8,128)(...) while((s32[]{:T(128)}, f32[4,12,128]{2,1,0:T(8,128)}, ...), condition=%wide.region_13.14_spmd, body=%wide.region_5.13_spmd.sunk | while | flops 210290176 | bytes 26590460 | solution.py:71
  173.1 78.6 %while.144 = (s32[]{:T(128)}, f32[4,12,128]{2,1,0:T(8,128)}, f32[4,12,128]{2,1,0:T(8,128)}, f32[4,12,128,64]{2,3,1,0:T(8,128)}, s32[4,128]{1,0:T(4,128)}, /*inde...) while((s32[]{:T(128)}, f32[4,12,128]{2,1,0:T(8,128)}, ...), condition=%wide.region_12.12_spmd.clone, body=%wide.region_7.11_spmd.clone.sunk | while | flops 210242560 | bytes 13994827 | solution.py:159
  182.5 7.5 conditional.11
  202.2 7.5 conditional.11
  221.8 7.5 conditional.11
  241.5 7.5 conditional.11
  258.2 63.5 %while.144 = (s32[]{:T(128)}, f32[4,12,128]{2,1,0:T(8,128)}, f32[4,12,128]{2,1,0:T(8,128)}, f32[4,12,128,64]{2,3,1,0:T(8,128)}, s32[4,128]{1,0:T(4,128)}, /*inde...) while((s32[]{:T(128)}, f32[4,12,128]{2,1,0:T(8,128)}, ...), condition=%wide.region_12.12_spmd.clone, body=%wide.region_7.11_spmd.clone.sunk | while | flops 210242560 | bytes 13994827 | solution.py:159
  267.6 7.5 conditional.11
  311.4 7.5 conditional.11
  326.2 6.5 fusion.99
  332.7 8.7 add_convert_fusion
  366.8 35.6 %reduce-scatter.19.cloned.1.call-done = bf16[96,768]{1,0:T(8,128)(2,1)} async-done(((bf16[768,768]{1,0:T(8,128)(2,1)}), bf16[96,768]{1,0:T(8,128)(2,1)}) %reduce-scatter.19.cloned.1.call-update) | async-done | bytes 147472 | tf_op jit(solution)/shard_map/reduce_scatter | solution.py:378
  406.3 39.2 %reduce-scatter.23.cloned.1.call-done = bf16[144,768]{1,0:T(8,128)(2,1)} async-done(((bf16[1152,768]{1,0:T(8,128)(2,1)}), bf16[144,768]{1,0:T(8,128)(2,1)}) %reduce-scatter.23.cloned.1.call-update) | async-done | bytes 221200 | tf_op jit(solution)/shard_map/reduce_scatter | solution.py:384
  448.8 113.4 %while.141 = (s32[]{:T(128)}, f32[4,128,12,64]{1,3,2,0:T(8,128)}, bf16[4,1024,768]{1,2,0:T(8,128)(2,1)}, bf16[4,1024,768]{1,2,0:T(8,128)(2,1)}, s32[4,1,8]{2,0,1...) while((s32[]{:T(128)}, f32[4,128,12,64]{1,3,2,0:T(8,128)}, ...), condition=%wide.region_25.26_spmd, body=%wide.region_19.25_spmd.sunk | while | flops 307018240 | bytes 24179956 | solution.py:71
  448.8 6.0 constant_dynamic-slice_fusion.31
  456.2 56.6 %while.145 = (s32[]{:T(128)}, f32[4,128,12,64]{1,3,2,0:T(8,128)}, s32[4,128]{1,0:T(4,128)}, s32[4,512]{1,0:T(4,128)}, bf16[4,128,12,64]{1,3,2,0:T(8,128)(2,1)}, ...) while((s32[]{:T(128)}, f32[4,128,12,64]{1,3,2,0:T(8,128)}, ...), condition=%wide.region_24.24_spmd.clone, body=%wide.region_21.23_spmd.clone.sunk | while | flops 306970624 | bytes 11584307 | solution.py:339
  462.4 7.1 conditional.10
  476.5 7.1 conditional.10
  490.6 7.1 conditional.10
  504.7 7.2 conditional.10
  512.7 5.9 constant_dynamic-slice_fusion.31
  520.0 42.2 %while.145 = (s32[]{:T(128)}, f32[4,128,12,64]{1,3,2,0:T(8,128)}, s32[4,128]{1,0:T(4,128)}, s32[4,512]{1,0:T(4,128)}, bf16[4,128,12,64]{1,3,2,0:T(8,128)(2,1)}, ...) while((s32[]{:T(128)}, f32[4,128,12,64]{1,3,2,0:T(8,128)}, ...), condition=%wide.region_24.24_spmd.clone, body=%wide.region_21.23_spmd.clone.sunk | while | flops 306970624 | bytes 11584307 | solution.py:339
  526.2 7.1 conditional.10
  554.2 7.2 conditional.10
  562.9 23.7 %all_gather.65 = bf16[4,12,1024]{2,1,0:T(8,128)(2,1)S(1)} all-gather(bf16[4,12,128]{2,1,0:T(8,128)(2,1)S(1)} %convert_element_type.225), channel_id=1, replica_groups=mesh['row'=4,'blk'=8] {'blk'}, dimensions={2}, use_global_device_ids=true | all-gather | bytes 110592 | tf_op jit(solution)/shard_map/all_gather | solution.py:213
  587.4 8.7 all_gather.64
  601.7 159.6 %while.143 = (s32[]{:T(128)}, f32[4,128,12,64]{1,3,2,0:T(8,128)}, f32[4,128,12,64]{1,3,2,0:T(8,128)}, bf16[4,1024,768]{1,2,0:T(8,128)(2,1)}, bf16[4,1024,768]{2,...) while((s32[]{:T(128)}, f32[4,128,12,64]{1,3,2,0:T(8,128)}, ...), condition=%wide.region_32.33_spmd, body=%wide.region_26.32_spmd.sunk | while | flops 410925568 | bytes 37380408 | solution.py:71
  612.8 80.3 %while.146 = (s32[]{:T(128)}, f32[4,128,12,64]{1,3,2,0:T(8,128)}, f32[4,128,12,64]{1,3,2,0:T(8,128)}, s32[4,512]{1,0:T(4,128)S(1)}, s32[4,128]{1,0:T(4,128)}, /*...) while((s32[]{:T(128)}, f32[4,128,12,64]{1,3,2,0:T(8,128)}, ...), condition=%wide.region_31.31_spmd.clone, body=%wide.region_28.30_spmd.clone.sunk | while | flops 410877952 | bytes 18100060 | solution.py:264
  618.7 11.6 %conditional.9 = (f32[1,128,12,64]{1,3,2,0:T(8,128)}, f32[1,128,12,64]{1,3,2,0:T(8,128)S(1)}) conditional(s32[]{:T(128)} %bitcast.238, (f32[128,12,64]{0,2,1:T(8,128)}, f32[128,12,64]{0,2,1:T(8,128)S(1)}) %tuple.356, (s32[1,512]{1,0:T(1,128)S(1)}, s32[1,128]{1,0:T(1,128)S(1)}, bf16[4,512,12,64]{1,3,2,0:T(8,128)(2,1)}, s32[]{:T(128)}, ...), branch_computations={%region_29.28_spmd, %region_30.29_spmd} | conditional | flops 410877952 | bytes 14947860 | solution.py:260
  638.8 11.7 %conditional.9 = (f32[1,128,12,64]{1,3,2,0:T(8,128)}, f32[1,128,12,64]{1,3,2,0:T(8,128)S(1)}) conditional(s32[]{:T(128)} %bitcast.238, (f32[128,12,64]{0,2,1:T(8,128)}, f32[128,12,64]{0,2,1:T(8,128)S(1)}) %tuple.356, (s32[1,512]{1,0:T(1,128)S(1)}, s32[1,128]{1,0:T(1,128)S(1)}, bf16[4,512,12,64]{1,3,2,0:T(8,128)(2,1)}, s32[]{:T(128)}, ...), branch_computations={%region_29.28_spmd, %region_30.29_spmd} | conditional | flops 410877952 | bytes 14947860 | solution.py:260
  658.9 11.6 %conditional.9 = (f32[1,128,12,64]{1,3,2,0:T(8,128)}, f32[1,128,12,64]{1,3,2,0:T(8,128)S(1)}) conditional(s32[]{:T(128)} %bitcast.238, (f32[128,12,64]{0,2,1:T(8,128)}, f32[128,12,64]{0,2,1:T(8,128)S(1)}) %tuple.356, (s32[1,512]{1,0:T(1,128)S(1)}, s32[1,128]{1,0:T(1,128)S(1)}, bf16[4,512,12,64]{1,3,2,0:T(8,128)(2,1)}, s32[]{:T(128)}, ...), branch_computations={%region_29.28_spmd, %region_30.29_spmd} | conditional | flops 410877952 | bytes 14947860 | solution.py:260
  679.0 11.6 %conditional.9 = (f32[1,128,12,64]{1,3,2,0:T(8,128)}, f32[1,128,12,64]{1,3,2,0:T(8,128)S(1)}) conditional(s32[]{:T(128)} %bitcast.238, (f32[128,12,64]{0,2,1:T(8,128)}, f32[128,12,64]{0,2,1:T(8,128)S(1)}) %tuple.356, (s32[1,512]{1,0:T(1,128)S(1)}, s32[1,128]{1,0:T(1,128)S(1)}, bf16[4,512,12,64]{1,3,2,0:T(8,128)(2,1)}, s32[]{:T(128)}, ...), branch_computations={%region_29.28_spmd, %region_30.29_spmd} | conditional | flops 410877952 | bytes 14947860 | solution.py:260
  704.3 57.0 %while.146 = (s32[]{:T(128)}, f32[4,128,12,64]{1,3,2,0:T(8,128)}, f32[4,128,12,64]{1,3,2,0:T(8,128)}, s32[4,512]{1,0:T(4,128)S(1)}, s32[4,128]{1,0:T(4,128)}, /*...) while((s32[]{:T(128)}, f32[4,128,12,64]{1,3,2,0:T(8,128)}, ...), condition=%wide.region_31.31_spmd.clone, body=%wide.region_28.30_spmd.clone.sunk | while | flops 410877952 | bytes 18100060 | solution.py:264
  710.1 11.6 %conditional.9 = (f32[1,128,12,64]{1,3,2,0:T(8,128)}, f32[1,128,12,64]{1,3,2,0:T(8,128)S(1)}) conditional(s32[]{:T(128)} %bitcast.238, (f32[128,12,64]{0,2,1:T(8,128)}, f32[128,12,64]{0,2,1:T(8,128)S(1)}) %tuple.356, (s32[1,512]{1,0:T(1,128)S(1)}, s32[1,128]{1,0:T(1,128)S(1)}, bf16[4,512,12,64]{1,3,2,0:T(8,128)(2,1)}, s32[]{:T(128)}, ...), branch_computations={%region_29.28_spmd, %region_30.29_spmd} | conditional | flops 410877952 | bytes 14947860 | solution.py:260
  747.1 11.6 %conditional.9 = (f32[1,128,12,64]{1,3,2,0:T(8,128)}, f32[1,128,12,64]{1,3,2,0:T(8,128)S(1)}) conditional(s32[]{:T(128)} %bitcast.238, (f32[128,12,64]{0,2,1:T(8,128)}, f32[128,12,64]{0,2,1:T(8,128)S(1)}) %tuple.356, (s32[1,512]{1,0:T(1,128)S(1)}, s32[1,128]{1,0:T(1,128)S(1)}, bf16[4,512,12,64]{1,3,2,0:T(8,128)(2,1)}, s32[]{:T(128)}, ...), branch_computations={%region_29.28_spmd, %region_30.29_spmd} | conditional | flops 410877952 | bytes 14947860 | solution.py:260
  781.4 6.3 fusion.129
  787.6 34.2 %all-reduce.5 = (bf16[768]{0:T(1024)(128)(2,1)S(1)}, bf16[768]{0:T(1024)(128)(2,1)S(1)}) all-reduce(bf16[768]{0:T(1024)(128)(2,1)S(1)} %get-tuple-element.1505, bf16[768]{0:T(1024)(128)(2,1)S(1)} %copy-done.33), channel_id=2, replica_groups=mesh['row'=4,'blk'=8] {'blk'}, use_global_device_ids=true, to_apply=%region_36.37.clone | all-reduce | flops 1536 | bytes 6144
  822.0 20.4 %reduce-scatter.17.cloned.1.call-done = bf16[96,2304]{1,0:T(8,128)(2,1)} async-done(((bf16[768,2304]{1,0:T(8,128)(2,1)}), bf16[96,2304]{1,0:T(8,128)(2,1)}) %reduce-scatter.17.cloned.1.call-update) | async-done | bytes 442384 | tf_op jit(solution)/shard_map/reduce_scatter | solution.py:375
  844.5 12.2 %all-reduce.4 = (f32[96]{0:T(128)}, f32[96]{0:T(128)}) all-reduce(f32[96]{0:T(128)S(1)} %dynamic-slice_convert_fusion.1, f32[96]{0:T(128)S(1)} %dynamic-slice_convert_fusion), channel_id=1, replica_groups=mesh['row'=4,'blk'=8] {'row'}, use_global_device_ids=true, to_apply=%region_37.38 | all-reduce | flops 192 | bytes 1536 | tf_op jit(solution)/shard_map/psum | solution.py:408
  859.6 7.0 reduce-scatter.25.cloned.1.call-done
  (477 shorter events, 454.0 us)
Async XLA Ops:
  7.2 18.9 %copy-start.32 = (u32[32]{0:T(128)S(1)}, u32[32]{0:T(128)}, u32[]{:S(2)}) copy-start(u32[32]{0:T(128)} %constant.388) | copy-start | bytes 388
  7.2 20.2 %copy-start.35 = (bf16[96]{0:T(256)(128)(2,1)S(1)}, bf16[96]{0:T(256)(128)(2,1)}, u32[]{:S(2)}) copy-start(bf16[96]{0:T(256)(128)(2,1)} %param.29) | copy-start | bytes 580
  7.2 20.4 %copy-start.36 = (bf16[96]{0:T(256)(128)(2,1)S(1)}, bf16[96]{0:T(256)(128)(2,1)}, u32[]{:S(2)}) copy-start(bf16[96]{0:T(256)(128)(2,1)} %param.32) | copy-start | bytes 580
  7.2 32.6 %copy-start.5 = (bf16[4,128,768]{2,1,0:T(8,128)(2,1)S(1)}, bf16[4,128,768]{2,1,0:T(8,128)(2,1)}, u32[]{:S(2)}) copy-start(bf16[4,128,768]{2,1,0:T(8,128)(2,1)} %param.27) | copy-start | bytes 2359300
  7.2 54.8 %all-gather.12.cloned.1.call-start = ((), (), s32[]{:S(2)}) async-start(), calls=%async_computation.8 | async-start | bytes 3981312 | tf_op jit(solution)/shard_map/all_gather | solution.py:93
  26.0 104.7 %all-gather.16.cloned.1.call-start = ((), (), s32[]{:S(2)}) async-start(), calls=%async_computation.10 | async-start | bytes 7077888 | tf_op jit(solution)/shard_map/all_gather | solution.py:170
  39.8 26.3 %copy-start.27 = (f32[768]{0:T(1024)}, f32[768]{0:T(1024)S(1)}, u32[]{:S(2)}) copy-start(f32[768]{0:T(1024)S(1)} %convert_element_type.204) | copy-start | bytes 9220
  40.0 26.1 %copy-start.24 = (f32[4,128]{1,0:T(4,128)}, f32[4,128]{1,0:T(4,128)S(1)}, u32[]{:S(2)}) copy-start(f32[4,128]{1,0:T(4,128)S(1)} %broadcast_multiply_fusion.6) | copy-start | bytes 6148
  40.4 25.8 %copy-start.29 = (f32[4,128]{1,0:T(4,128)}, f32[4,128]{1,0:T(4,128)S(1)}, u32[]{:S(2)}) copy-start(f32[4,128]{1,0:T(4,128)S(1)} %add_rsqrt_fusion.1) | copy-start | bytes 6148
  66.1 2.2 copy-start.12
  69.3 94.8 %all-gather.14.cloned.1.call-start = ((), (), s32[]{:S(2)}) async-start(), calls=%async_computation.9 | async-start | bytes 7077888 | tf_op jit(solution)/shard_map/all_gather | solution.py:169
  80.3 15.7 %copy-start.21 = (bf16[96,576]{1,0:T(8,128)(2,1)S(1)}, bf16[96,576]{1,0:T(8,128)(2,1)}, u32[]{:S(2)}) copy-start(bf16[96,576]{1,0:T(8,128)(2,1)} %param.33) | copy-start | bytes 331780
  81.3 32.4 %copy-start.22 = (bf16[144,192]{1,0:T(8,128)(2,1)S(1)}, bf16[144,192]{1,0:T(8,128)(2,1)}, u32[]{:S(2)}) copy-start(bf16[144,192]{1,0:T(8,128)(2,1)} %param.34) | copy-start | bytes 165892
  81.3 242.1 %all-gather.18.cloned.1.call-start = ((), (), s32[]{:S(2)}) async-start(), calls=%async_computation.11 | async-start | bytes 1327104 | tf_op jit(solution)/shard_map/all_gather | solution.py:94
  96.0 33.7 %copy-start.15 = (bf16[4,128,12,32]{1,3,2,0:T(8,128)(2,1)S(1)}, bf16[4,128,12,32]{1,3,2,0:T(8,128)(2,1)}, u32[]{:S(2)}) copy-start(bf16[4,128,12,32]{1,3,2,0:T(8,128)(2,1)} %get-tuple-element.1686) | copy-start | bytes 1179652
  96.0 230.2 %all-gather.20.cloned.1.call-start = ((), (), s32[]{:S(2)}) async-start(), calls=%async_computation.12 | async-start | bytes 3981312 | tf_op jit(solution)/shard_map/all_gather | solution.py:95
  113.6 219.1 %all-gather.22.cloned.1.call-start = ((), (), s32[]{:S(2)}) async-start(), calls=%async_computation.13 | async-start | bytes 1990656 | tf_op jit(solution)/shard_map/all_gather | solution.py:96
  128.9 273.5 %reduce-scatter.19.cloned.1.call-start = ((), (), s32[]{:S(2)}) async-start(), calls=%async_computation.17 | async-start | bytes 1327104 | tf_op jit(solution)/shard_map/reduce_scatter | solution.py:378
  321.7 1.7 copy-start.6
  323.4 2.8 copy-start.9
  323.4 2.8 copy-start.26
  325.8 28.6 %copy-start.3 = (f32[4,128,768]{2,1,0:T(8,128)}, f32[4,128,768]{2,1,0:T(8,128)S(1)}, u32[]{:S(2)}) copy-start(f32[4,128,768]{2,1,0:T(8,128)S(1)} %get-tuple-element.1699) | copy-start | bytes 4718596
  326.2 6.5 copy-start.19
  332.7 8.8 copy-start.11
  341.4 1.6 copy-start.37
  341.4 3.3 copy-start.34
  343.1 4.4 copy-start.17
  344.7 2.8 copy-start.20
  348.6 12.0 %copy-start.1 = (f32[4,128,768]{2,1,0:T(8,128)}, f32[4,128,768]{2,1,0:T(8,128)S(1)}, u32[]{:S(2)}) copy-start(f32[4,128,768]{2,1,0:T(8,128)S(1)} %multiply_add_fusion) | copy-start | bytes 4718596
  350.5 95.1 %reduce-scatter.23.cloned.1.call-start = ((), (), s32[]{:S(2)}) async-start(), calls=%async_computation.19 | async-start | bytes 1990656 | tf_op jit(solution)/shard_map/reduce_scatter | solution.py:384
  354.4 242.4 %reduce-scatter.21.cloned.1.call-start = ((), (), s32[]{:S(2)}) async-start(), calls=%async_computation.18 | async-start | bytes 3981312 | tf_op jit(solution)/shard_map/reduce_scatter | solution.py:381
  360.0 238.9 %all-gather.24.cloned.1.call-start = ((), (), s32[]{:S(2)}) async-start(), calls=%async_computation.14 | async-start | bytes 7077888 | tf_op jit(solution)/shard_map/all_gather | solution.py:281
  360.6 2.5 copy-start.8
  360.6 238.3 %all-gather.26.cloned.1.call-start = ((), (), s32[]{:S(2)}) async-start(), calls=%async_computation.15 | async-start | bytes 7077888 | tf_op jit(solution)/shard_map/all_gather | solution.py:282
  363.0 41.2 %copy-start = (f32[4,12,128,64]{2,3,1,0:T(8,128)S(1)}, f32[4,12,128,64]{2,3,1,0:T(8,128)}, u32[]{:S(2)}) copy-start(f32[4,12,128,64]{2,3,1,0:T(8,128)} %get-tuple-element.1281) | copy-start | bytes 4718596
  363.0 413.3 %reduce-scatter.27.cloned.1.call-start = ((), (), s32[]{:S(2)}) async-start(), calls=%async_computation.21 | async-start | bytes 245760
  404.1 373.8 %reduce-scatter.31.cloned.1.call-start = ((), (), s32[]{:S(2)}) async-start(), calls=%async_computation.23 | async-start | bytes 491520
  447.5 332.1 %reduce-scatter.29.cloned.1.call-start = ((), (), s32[]{:S(2)}) async-start(), calls=%async_computation.22 | async-start | bytes 737280
  598.9 243.5 %reduce-scatter.17.cloned.1.call-start = ((), (), s32[]{:S(2)}) async-start(), calls=%async_computation.16 | async-start | bytes 3981312 | tf_op jit(solution)/shard_map/reduce_scatter | solution.py:375
  765.2 1.8 copy-start.7
  765.2 1.8 copy-start.25
  765.3 1.8 copy-start.28
  765.3 1.7 copy-start.30
  765.6 1.4 copy-start.14
  771.1 1.8 copy-start.16
  771.1 95.5 %reduce-scatter.25.cloned.1.call-start = ((), (), s32[]{:S(2)}) async-start(), calls=%async_computation.20 | async-start | bytes 737280
  781.4 6.3 copy-start.33
  787.6 69.1 %copy-start.2 = (f32[4,128,768]{2,1,0:T(8,128)S(1)}, f32[4,128,768]{2,1,0:T(8,128)}, u32[]{:S(2)}) copy-start(f32[4,128,768]{2,1,0:T(8,128)} %copy-done.1) | copy-start | bytes 4718596
  (6 other events, 7.2 us)
Sparse Core Ops, SparseCore 0:
  26.2 35.7 all-gather.11
  69.4 45.5 all-gather.15
  117.4 46.6 all-gather.13
  166.4 24.0 all-gather.17
  192.3 33.9 all-gather.19
  228.6 26.5 all-gather.21
  350.6 51.7 reduce-scatter.18
  406.1 39.3 reduce-scatter.22
  449.4 48.0 reduce-scatter.20
  499.4 46.6 all-gather.23
  548.2 46.1 all-gather.25
  597.1 19.4 reduce-scatter.26
  618.9 18.7 reduce-scatter.30
  640.0 20.2 reduce-scatter.28
  771.2 71.1 reduce-scatter.16
  844.6 21.9 reduce-scatter.24
where the time goes:
time: 891 us; the launch traced here: 875 us
  local copies, waits for them, and re-layouts  267 us (30%)
  matrix products  162 us (18%)
  blocking collectives  152 us (17%)
  waiting for transfers between devices  149 us (17%)
  other arithmetic  65.9 us (7%)
  loops' own time  62.4 us (7%)
  between operations  16.5 us (2%)
    unnamed x2, blocking collectives  46.2 us
    reduce_scatter x1, waiting for transfers between devices, body(): lax.psum_scatter(grad_down.astype(jnp.bfloat16), 'blk', scatter_dimension...  39.2 us
    reduce_scatter x1, waiting for transfers between devices, body(): lax.psum_scatter(grad_out.astype(jnp.bfloat16), 'blk', scatter_dimension=...  35.6 us
    dynamic_slice x48, local copies, waits for them, and re-layouts, attend(): lax.map(attend_per_row, (state, queries, query_docs, block_keys, block_va...  35.3 us
    squeeze x22, local copies, waits for them, and re-layouts, key_grads(): lax.map(key_per_row, (state, block_queries, block_dout, block_lse, block_...  32.2 us
    dot_general x6, matrix products, key_accumulate(): jnp.einsum('hqk,qhd->khd', dscores, row_bq, preferred_element_type=jnp.fl...  28.1 us
    dynamic_update_slice x24, local copies, waits for them, and re-layouts, key_grads(): lax.map(key_per_row, (state, block_queries, block_dout, block_lse, block_...  27.1 us
    slice x24, local copies, waits for them, and re-layouts, row_intersections(): return (query_docs[0] <= key_docs[-1]) & (key_docs[0] <= query_docs[-1])  26.7 us
  transfers between devices with their start and end apart: 16, of which 6 were waited for; matrix products, arithmetic and copies ran while one was open for 53% of the time, Pallas kernels for 0%

commit v1 on v0

v1 whole, which is shorter than its diff:
```python
import functools
import math

import jax
import jax.numpy as jnp
import numpy as np
from jax import lax
from jax.experimental import pallas as pl
from jax.experimental.pallas import tpu as pltpu
from jax.sharding import PartitionSpec as P

D = 768
HEADS = 12
HD = 64
FF = 1152
NDOC = 8
PAIRS = HEADS // 2
EXT = 3 * D + 128

ROPE_BASE = 160000.0
NORM_EPSILON = 1e-05
MASKED = -1e30
F32 = jnp.float32
BF16 = jnp.bfloat16
NN = (((1,), (0,)), ((), ()))
NT = (((1,), (1,)), ((), ()))
TN = (((0,), (0,)), ((), ()))
VMEM_BYTES = 56 * 1024 * 1024
SMEM = pl.BlockSpec(memory_space=pltpu.SMEM)
ANY = pl.BlockSpec(memory_space=pl.ANY)
VMEM = pl.BlockSpec(memory_space=pltpu.VMEM)


def dot(a, b, dims):
    return lax.dot_general(a, b, dims, preferred_element_type=F32)


def shape_of(dims, dtype):
    return jax.ShapeDtypeStruct(tuple(dims), dtype)


def params():
    return pltpu.CompilerParams(vmem_limit_bytes=VMEM_BYTES)


def cost(flops, moved, exps=0):
    return pl.CostEstimate(flops=int(flops), bytes_accessed=int(moved), transcendentals=int(exps))


class Plan:
    def __init__(self, mesh, rows, tok):
        self.nrow = mesh.shape["row"]
        self.nblk = mesh.shape["blk"]
        self.rows = rows
        self.tok = tok
        self.local = rows * tok
        self.chips = self.nblk // 2
        self.bits = self.chips.bit_length() - 1
        self.groups = self.nblk // rows
        self.r = D // self.nblk
        self.rf = FF // self.nblk
        self.cw = D // self.nrow
        self.aligned = self.r % 16 == 0 and self.rf % 16 == 0
        self.packed = 4 * self.r + self.rf
        rows_, chips, nrow = self.rows, self.chips, self.nrow
        self.at_pick = 0
        self.at_base = self.at_pick + rows_
        self.at_own = self.at_base + self.groups * rows_
        self.at_other = self.at_own + chips
        self.at_z = self.at_other + chips
        self.at_lo = self.at_z + nrow
        self.size = self.at_lo + 1
        table = np.zeros((nrow, self.nblk, self.size), np.int32)
        for z in range(nrow):
            for blk in range(self.nblk):
                chip, core = blk // 2, blk % 2
                low = chip % rows_
                entry = table[z, blk]
                for j in range(rows_):
                    entry[self.at_pick + j] = low ^ j
                for e in range(self.groups):
                    other = blk ^ self.member(e)
                    for j in range(rows_):
                        entry[self.at_base + e * rows_ + j] = (2 * ((other // 2) ^ j) + other % 2) * tok
                for j in range(chips):
                    entry[self.at_own + j] = 2 * (chip ^ self.order(core, j)) + core
                    entry[self.at_other + j] = 2 * (chip ^ self.order(1 - core, j)) + 1 - core
                for other in range(nrow):
                    entry[self.at_z + other] = other ^ z
                entry[self.at_lo] = low
        self.table = table

    def member(self, e):
        return (e & 1) | ((e >> 1) * 2 * self.rows)

    def order(self, core, j):
        if core == 0:
            return j
        return int(format(j, "0%db" % self.bits)[::-1], 2) if self.bits else 0

    def step_pairs(self, step):
        def flip(blk):
            bit = step if blk % 2 == 0 else self.bits - 1 - step
            return 2 * ((blk // 2) ^ (1 << bit)) + blk % 2

        return [(blk, flip(blk)) for blk in range(self.nblk)]

    def xor_pairs(self, mask):
        return [(blk, blk ^ mask) for blk in range(self.nblk)]

    def z_pairs(self, mask):
        return [(z, z ^ mask) for z in range(self.nrow)]


def swap_cores(plan, value):
    return lax.ppermute(value, "blk", plan.xor_pairs(1))


def gather_z(plan, value):
    return [value] + [lax.ppermute(value, "row", plan.z_pairs(j)) for j in range(1, plan.nrow)]


def exchange_rows(plan, pieces):
    return [pieces[0]] + [
        lax.ppermute(pieces[j], "blk", plan.xor_pairs(2 * j)) for j in range(1, plan.rows)
    ]


def gather_xy(plan, value):
    pieces = [value]
    others = [swap_cores(plan, value)]
    for step in range(plan.bits):
        pairs = plan.step_pairs(step)
        more = [lax.ppermute(piece, "blk", pairs) for piece in pieces]
        pieces = pieces + more
        others = others + [swap_cores(plan, piece) for piece in more]
    return pieces, others


def add_low(a, b):
    return (a.astype(F32) + b.astype(F32)).astype(BF16)


def reduce_xy(plan, keep, send):
    half = plan.chips // 2
    if half == 0:
        return add_low(keep, swap_cores(plan, send))[0]
    high = add_low(keep[half:], swap_cores(plan, send[half:]))
    total = add_low(keep[:half], swap_cores(plan, send[:half]))
    for step in reversed(range(plan.bits)):
        moved = lax.ppermute(high, "blk", plan.step_pairs(step))
        half = half // 2
        if step == 0:
            return add_low(total, moved)[0]
        high = add_low(total[half:], moved[half:])
        total = add_low(total[:half], moved[:half])


def layer_norm(values):
    average = jnp.mean(values, axis=-1, keepdims=True)
    centred = values - average
    inv_std = lax.rsqrt(jnp.mean(centred * centred, axis=-1, keepdims=True) + NORM_EPSILON)
    return centred * inv_std, inv_std


def norm_backward(grad_out, normalized, inv_std, gain):
    scaled = grad_out * gain
    inner = jnp.mean(scaled * normalized, axis=-1, keepdims=True)
    outer = jnp.mean(scaled, axis=-1, keepdims=True)
    return inv_std * (scaled - outer - normalized * inner)


def swap_halves(values):
    lane = lax.broadcasted_iota(jnp.int32, values.shape, 1)
    width = values.shape[1]
    half = HD // 2
    return jnp.where(
        (lane & half) == 0, pltpu.roll(values, width - half, 1), pltpu.roll(values, half, 1)
    )


def rotate_pair(values, cosine, sine, direction):
    return values * cosine + swap_halves(values) * (direction * sine)


def rotate_all(values, cosine, sine, direction):
    return jnp.concatenate(
        [
            rotate_pair(values[:, 128 * p : 128 * (p + 1)], cosine, sine, direction)
            for p in range(PAIRS)
        ],
        axis=1,
    )


def pick_kernel(plan, meta, tokens, cotangent, *refs):
    outs, sems = refs[: plan.rows], refs[plan.rows]
    copies = []
    for j in range(plan.rows):
        row = meta[plan.at_pick + j]
        copies.append(pltpu.make_async_copy(tokens.at[row], outs[j].at[0], sems.at[2 * j]))
        copies.append(pltpu.make_async_copy(cotangent.at[row], outs[j].at[1], sems.at[2 * j + 1]))
    for copy in copies:
        copy.start()
    for copy in copies:
        copy.wait()


def pick(plan, meta, tokens, cotangent):
    return pl.pallas_call(
        functools.partial(pick_kernel, plan),
        in_specs=[SMEM, ANY, ANY],
        out_specs=[ANY] * plan.rows,
        out_shape=[shape_of((2, plan.tok, D), BF16)] * plan.rows,
        scratch_shapes=[pltpu.SemaphoreType.DMA((2 * plan.rows,))],
        compiler_params=params(),
        cost_estimate=cost(0, 4 * plan.local * D * 2),
        name="pick_rows",
    )(meta, tokens, cotangent)


def place_kernel(plan, meta, *refs):
    pieces, out, sems = refs[: plan.rows], refs[plan.rows], refs[plan.rows + 1]
    copies = []
    for j in range(plan.rows):
        row = meta[plan.at_pick + j]
        copies.append(pltpu.make_async_copy(pieces[j], out.at[row], sems.at[j]))
    for copy in copies:
        copy.start()
    for copy in copies:
        copy.wait()


def place(plan, meta, pieces):
    return pl.pallas_call(
        functools.partial(place_kernel, plan),
        in_specs=[SMEM] + [ANY] * plan.rows,
        out_specs=ANY,
        out_shape=shape_of((plan.rows, plan.tok, D), BF16),
        scratch_shapes=[pltpu.SemaphoreType.DMA((plan.rows,))],
        compiler_params=params(),
        cost_estimate=cost(0, 2 * plan.local * D * 2),
        name="place_rows",
    )(meta, *pieces)


def ordered(plan, meta, pieces):
    stacked = jnp.stack(pieces)
    return [
        lax.dynamic_index_in_dim(stacked, meta[plan.at_z + z], 0, keepdims=False)
        for z in range(plan.nrow)
    ]


def join_qkv_kernel(plan, meta, gains, *refs):
    pieces, out, held = refs[: plan.nrow], refs[plan.nrow], refs[plan.nrow + 1]
    width = 3 * plan.cw
    for j in range(plan.nrow):
        held[j] = pieces[j][...]
    for z in range(plan.nrow):
        out[:, width * z : width * (z + 1)] = held[meta[plan.at_z + z]]
    out[:, 3 * D :] = gains[...]


def join_qkv(plan, meta, gains, pieces):
    if not plan.aligned:
        return jnp.concatenate(ordered(plan, meta, pieces) + [gains], axis=1)
    return pl.pallas_call(
        functools.partial(join_qkv_kernel, plan),
        in_specs=[SMEM] + [VMEM] * (1 + plan.nrow),
        out_specs=VMEM,
        out_shape=shape_of((plan.r, EXT), BF16),
        scratch_shapes=[pltpu.VMEM((plan.nrow, plan.r, 3 * plan.cw), BF16)],
        compiler_params=params(),
        cost_estimate=cost(0, 2 * plan.r * EXT * 2),
        name="join_qkv",
    )(meta, gains, *pieces)


def pack_rest(plan, w_out, w_in, w_down):
    cw = plan.cw
    left = jnp.concatenate([w_in[:, :cw], w_in[:, cw : 2 * cw], w_out], axis=0)
    blank = jnp.zeros((2 * plan.r - plan.rf, cw), BF16)
    right = jnp.concatenate([w_in[:, 2 * cw :], w_down, blank], axis=0)
    return jnp.concatenate([left, right], axis=1)


def unpack_rest(plan, piece):
    r, rf, cw = plan.r, plan.rf, plan.cw
    parts_in = [piece[:r, :cw], piece[r : 2 * r, :cw], piece[:r, cw:]]
    return parts_in, piece[2 * r : 3 * r, :cw], piece[r : r + rf, cw:]


def join_rest_kernel(plan, meta, *refs):
    pieces, out, held = refs[: plan.nrow], refs[plan.nrow], refs[plan.nrow + 1]
    r, cw = plan.r, plan.cw
    for j in range(plan.nrow):
        held[j] = pieces[j][...]
    for z in range(plan.nrow):
        parts_in, part_out, part_down = unpack_rest(plan, held[meta[plan.at_z + z]])
        out[:r, cw * z : cw * (z + 1)] = part_out
        for i in range(3):
            block, place_at = (3 * z + i) // plan.nrow, (3 * z + i) % plan.nrow
            out[r * (1 + block) : r * (2 + block), cw * place_at : cw * (place_at + 1)] = parts_in[i]
        out[4 * r :, cw * z : cw * (z + 1)] = part_down


def join_rest(plan, meta, pieces):
    if not plan.aligned:
        parts = [unpack_rest(plan, piece) for piece in ordered(plan, meta, pieces)]
        w_in = jnp.concatenate([part for item in parts for part in item[0]], axis=1)
        blocks = [jnp.concatenate([item[1] for item in parts], axis=1)]
        blocks += [w_in[:, D * t : D * (t + 1)] for t in range(3)]
        blocks += [jnp.concatenate([item[2] for item in parts], axis=1)]
        return jnp.concatenate(blocks, axis=0)
    return pl.pallas_call(
        functools.partial(join_rest_kernel, plan),
        in_specs=[SMEM] + [VMEM] * plan.nrow,
        out_specs=VMEM,
        out_shape=shape_of((plan.packed, D), BF16),
        scratch_shapes=[pltpu.VMEM((plan.nrow, 3 * plan.r, 2 * plan.cw), BF16)],
        compiler_params=params(),
        cost_estimate=cost(0, 2 * plan.packed * D * 2),
        name="join_rest",
    )(meta, *pieces)


def by_block(plan, meta, own, other):
    stacked = jnp.stack(own + other)
    places = meta[plan.at_own : plan.at_other + plan.chips]
    return jnp.zeros_like(stacked).at[places].set(stacked)


def split_blocks(plan, meta, blocks):
    own = jnp.take(blocks, meta[plan.at_own : plan.at_own + plan.chips], axis=0)
    other = jnp.take(blocks, meta[plan.at_other : plan.at_other + plan.chips], axis=0)
    return own, other


def qkv_sources(plan, meta, own, other):
    if plan.aligned:
        return own + other
    return [by_block(plan, meta, own, other).reshape(D, EXT)]


def rest_sources(plan, meta, own, other):
    if plan.aligned:
        return own + other
    blocks = by_block(plan, meta, own, other)
    r = plan.r
    parts = [blocks[:, r * i : r * (i + 1)].reshape(D, D) for i in range(4)]
    parts.append(blocks[:, 4 * r :].reshape(FF, D))
    return [jnp.concatenate(parts, axis=0)]


def block_size(plan):
    return (plan.r, plan.rf) if plan.aligned else (D, FF)


def block_of(plan, meta, index):
    return meta[plan.at_own + index] if plan.aligned else 0


def rows_at(index, size):
    if isinstance(index, int):
        return pl.ds(index * size, size)
    return pl.ds(pl.multiple_of(index * size, size), size)


def qkv_copies(plan, meta, sources, w_ref, sems):
    r, _ = block_size(plan)
    return [
        pltpu.make_async_copy(source, w_ref.at[rows_at(block_of(plan, meta, i), r)], sems.at[i])
        for i, source in enumerate(sources)
    ]


def rest_copies(plan, meta, sources, w_out, w_in, w_down, sems):
    r, rf = block_size(plan)
    found = [[], [], []]
    for i, source in enumerate(sources):
        block = block_of(plan, meta, i)
        rows = rows_at(block, r)
        found[0].append(
            pltpu.make_async_copy(source.at[pl.ds(0, r)], w_out.at[rows], sems.at[5 * i])
        )
        for t in range(3):
            found[1].append(
                pltpu.make_async_copy(
                    source.at[pl.ds((1 + t) * r, r)], w_in.at[t, rows], sems.at[5 * i + 1 + t]
                )
            )
        found[2].append(
            pltpu.make_async_copy(
                source.at[pl.ds(4 * r, rf)], w_down.at[rows_at(block, rf)], sems.at[5 * i + 4]
            )
        )
    return found


def source_count(plan):
    return 2 * plan.chips if plan.aligned else 1


def qkv_kernel(plan, meta, cos_ref, sin_ref, *refs):
    x_refs = refs[: plan.rows]
    count = source_count(plan)
    sources = refs[plan.rows : plan.rows + count]
    q_ref, kv_ref, n_ref, gain_ref, w_ref, sems = refs[plan.rows + count :]
    copies = qkv_copies(plan, meta, sources, w_ref, sems)
    for copy in copies:
        copy.start()
    units = [layer_norm(x_refs[j][0].astype(F32))[0] for j in range(plan.rows)]
    for copy in copies:
        copy.wait()
    gain_ref[...] = w_ref[:, 3 * D :].astype(F32).T[:8, :]
    for j in range(plan.rows):
        n_ref[plan.tok * j : plan.tok * (j + 1), :] = (units[j] * gain_ref[0:1, :]).astype(BF16)
    cosine, sine = cos_ref[...], sin_ref[...]
    normed = n_ref[...]
    queries = dot(normed, w_ref[:, :D], NN)
    q_ref[...] = rotate_all(queries, cosine, sine, 1.0).astype(BF16)
    keys = dot(normed, w_ref[:, D : 2 * D], NN)
    kv_ref[0] = rotate_all(keys, cosine, sine, 1.0).astype(BF16)
    kv_ref[1] = dot(normed, w_ref[:, 2 * D : 3 * D], NN).astype(BF16)


def project(plan, meta, cosine, sine, pieces, sources):
    local = plan.local
    count = len(sources)
    return pl.pallas_call(
        functools.partial(qkv_kernel, plan),
        in_specs=[SMEM, VMEM, VMEM] + [VMEM] * plan.rows + [ANY] * count,
        out_specs=[VMEM] * 4,
        out_shape=[
            shape_of((local, D), BF16),
            shape_of((2, local, D), BF16),
            shape_of((local, D), BF16),
            shape_of((8, D), F32),
        ],
        scratch_shapes=[pltpu.VMEM((D, EXT), BF16), pltpu.SemaphoreType.DMA((count,))],
        compiler_params=params(),
        cost_estimate=cost(2 * local * D * 3 * D, 2 * (D * EXT + 6 * local * D)),
        name="project",
    )(meta, cosine, sine, *pieces, *sources)


def fill_docs(plan, meta, lengths, kdoc, qdoc):
    low = meta[plan.at_lo]
    ends = []
    passed = jnp.int32(0)
    for n in range(NDOC):
        passed = passed + lengths[low, n]
        ends.append(passed)

    def docs(places):
        total = jnp.zeros(places.shape, jnp.int32)
        for end in ends:
            total = total + (places >= end).astype(jnp.int32)
        return total

    tok = plan.tok
    for i in range(plan.groups * plan.rows):
        first = meta[plan.at_base + i]
        kdoc[i * tok : (i + 1) * tok, :] = docs(
            first + lax.broadcasted_iota(jnp.int32, (tok, 128), 0)
        )
    for i in range(plan.rows):
        first = meta[plan.at_base + i]
        qdoc[:, i * tok : (i + 1) * tok] = docs(
            first + lax.broadcasted_iota(jnp.int32, (8, tok), 1)
        )


def head_part(pair, head):
    lane = lax.broadcasted_iota(jnp.int32, pair.shape, 1)
    keep = (lane < HD) if head == 0 else (lane >= HD)
    return jnp.where(keep, pair, jnp.zeros_like(pair))


def same_docs(kdoc, qdoc, first, size, q0, width):
    key_docs = jnp.concatenate([kdoc[first : first + size, :]] * (width // 128), axis=1)
    return key_docs == qdoc[0:1, q0 : q0 + width]


def attend_kernel(plan, width, meta, lengths, q_ref, *refs):
    groups, local = plan.groups, plan.local
    kv = refs[:groups]
    o_ref, low_ref, lse_ref, kdoc, qdoc, s_ref = refs[groups:]

    @pl.when(pl.program_id(0) == 0)
    def _():
        fill_docs(plan, meta, lengths, kdoc, qdoc)

    values_t = [kv[e][1].T for e in range(groups)]
    for first in range(0, local, width):
        rows = slice(first, first + width)
        queries = q_ref[rows, :] * jnp.asarray(1.0 / math.sqrt(HD), BF16)
        parts = []
        for h in range(2):
            head_queries = head_part(queries, h)
            top = jnp.full((1, width), MASKED, F32)
            for e in range(groups):
                scores = dot(kv[e][0], head_queries, NT)
                mask = same_docs(kdoc, qdoc, e * local, local, first, width)
                scores = jnp.where(mask, scores, MASKED)
                s_ref[h, e * local : (e + 1) * local, :] = scores
                top = jnp.maximum(top, jnp.max(scores, axis=0, keepdims=True))
            total = jnp.zeros((1, width), F32)
            weighted = jnp.zeros((HD, width), F32)
            for e in range(groups):
                probs = jnp.exp(s_ref[h, e * local : (e + 1) * local, :] - top)
                total = total + jnp.sum(probs, axis=0, keepdims=True)
                weighted = weighted + dot(
                    values_t[e][h * HD : (h + 1) * HD, :], probs.astype(BF16), NN
                )
            parts.append(weighted / total)
            lse_ref[0, h : h + 1, rows] = top + jnp.log(total)
        heads = jnp.concatenate(parts, axis=0).T
        o_ref[rows, :] = heads
        low_ref[rows, :] = heads.astype(BF16)


def attend(plan, meta, lengths, queries, kv):
    local, groups = plan.local, plan.groups
    width = min(512, local)
    pair = pl.BlockSpec((local, 128), lambda p: (0, p))
    pair_kv = pl.BlockSpec((2, local, 128), lambda p: (0, 0, p))
    return pl.pallas_call(
        functools.partial(attend_kernel, plan, width),
        grid=(PAIRS,),
        in_specs=[SMEM, SMEM, pair] + [pair_kv] * groups,
        out_specs=[pair, pair, pl.BlockSpec((1, 2, local), lambda p: (p, 0, 0))],
        out_shape=[
            shape_of((local, D), F32),
            shape_of((local, D), BF16),
            shape_of((PAIRS, 2, local), F32),
        ],
        scratch_shapes=[
            pltpu.VMEM((groups * local, 128), jnp.int32),
            pltpu.VMEM((8, local), jnp.int32),
            pltpu.VMEM((2, groups * local, width), F32),
        ],
        compiler_params=params(),
        cost_estimate=cost(16 * local * local * groups * D, 2 * local * D * (4 + 2 * groups)),
        name="attend",
    )(meta, lengths, queries, *kv)


def attend_back_kernel(
    plan, width, meta, lengths, q_ref, do_ref, o_ref, lse_ref, cos_ref, sin_ref, *refs
):
    groups, local = plan.groups, plan.local
    kv = refs[:groups]
    dq_ref = refs[groups]
    dkv = refs[groups + 1 : 2 * groups + 1]
    kdoc, qdoc, held = refs[2 * groups + 1 :]

    @pl.when(pl.program_id(0) == 0)
    def _():
        fill_docs(plan, meta, lengths, kdoc, qdoc)

    keys_t = [kv[e][0].T for e in range(groups)]
    scale = 1.0 / math.sqrt(HD)
    for first in range(0, local, width):
        rows = slice(first, first + width)
        queries = q_ref[rows, :] * jnp.asarray(scale, BF16)
        dout = do_ref[rows, :]
        product = (dout.astype(F32) * o_ref[rows, :]).T
        parts = []
        for h in range(2):
            head_queries = head_part(queries, h)
            head_dout = head_part(dout, h)
            lse = lse_ref[0, h : h + 1, rows]
            delta = jnp.sum(product[h * HD : (h + 1) * HD, :], axis=0, keepdims=True)
            grad_queries = jnp.zeros((HD, width), F32)
            for e in range(groups):
                scores = dot(kv[e][0], head_queries, NT)
                mask = same_docs(kdoc, qdoc, e * local, local, first, width)
                probs = jnp.exp(jnp.where(mask, scores, MASKED) - lse)
                dprobs = dot(kv[e][1], head_dout, NT)
                dscores = (probs * (dprobs - delta)).astype(BF16)
                grad_values = dot(probs.astype(BF16), head_dout, NN)
                grad_keys = dot(dscores, head_queries, NN)
                if first == 0 and h == 0:
                    held[e, 0] = grad_keys
                    held[e, 1] = grad_values
                else:
                    held[e, 0] += grad_keys
                    held[e, 1] += grad_values
                grad_queries = grad_queries + dot(
                    keys_t[e][h * HD : (h + 1) * HD, :], dscores, NN
                )
            parts.append(grad_queries)
        grad = jnp.concatenate(parts, axis=0).T * scale
        dq_ref[rows, :] = rotate_pair(grad, cos_ref[rows, :], sin_ref[rows, :], -1.0).astype(BF16)
    for e in range(groups):
        dkv[e][...] = held[e].astype(BF16)


def attend_back(plan, meta, lengths, queries, dout, heads, lse, cosine, sine, kv):
    local, groups = plan.local, plan.groups
    width = min(256, local)
    pair = pl.BlockSpec((local, 128), lambda p: (0, p))
    table = pl.BlockSpec((local, 128), lambda p: (0, 0))
    pair_kv = pl.BlockSpec((2, local, 128), lambda p: (0, 0, p))
    return pl.pallas_call(
        functools.partial(attend_back_kernel, plan, width),
        grid=(PAIRS,),
        in_specs=[
            SMEM,
            SMEM,
            pair,
            pair,
            pair,
            pl.BlockSpec((1, 2, local), lambda p: (p, 0, 0)),
            table,
            table,
        ]
        + [pair_kv] * groups,
        out_specs=[pair] + [pair_kv] * groups,
        out_shape=[shape_of((local, D), BF16)] + [shape_of((2, local, D), BF16)] * groups,
        scratch_shapes=[
            pltpu.VMEM((groups * local, 128), jnp.int32),
            pltpu.VMEM((8, local), jnp.int32),
            pltpu.VMEM((groups, 2, local, 128), F32),
        ],
        compiler_params=params(),
        cost_estimate=cost(40 * local * local * groups * D, 2 * local * D * (6 + 4 * groups)),
        name="attend_back",
    )(meta, lengths, queries, dout, heads, lse, cosine, sine, *kv)


def middle_kernel(plan, meta, low_ref, gain_ref, *refs):
    rows, tok, local = plan.rows, plan.tok, plan.local
    count = source_count(plan)
    x_refs = refs[:rows]
    sources = refs[rows : rows + count]
    refs = refs[rows + count :]
    out_refs = refs[:rows]
    do_ref, dh_ref, gain_grad_ref = refs[rows : rows + 3]
    grads = refs[rows + 3 : rows + 3 + (2 if plan.aligned else 1)]
    (
        w_out,
        w_in,
        w_down,
        h_ref,
        n_ref,
        gu_ref,
        mid_ref,
        dgu_ref,
        g_out,
        g_in,
        g_down,
        in_sems,
        out_sems,
    ) = refs[rows + 3 + len(grads) :]
    copies = rest_copies(plan, meta, sources, w_out, w_in, w_down, in_sems)
    for group in copies:
        for copy in group:
            copy.start()
    for copy in copies[0]:
        copy.wait()
    branch = dot(low_ref[...], w_out[...], NN)
    for j in range(rows):
        part = slice(tok * j, tok * (j + 1))
        h_ref[part, :] = x_refs[j][0].astype(F32) + branch[part, :]
    gain = gain_ref[1:2, :]
    unit, inv_std = layer_norm(h_ref[...])
    n_ref[...] = (unit * gain).astype(BF16)
    for copy in copies[1]:
        copy.wait()
    for t in range(3):
        gu_ref[:, D * t : D * (t + 1)] = dot(n_ref[...], w_in[t], NN)
    for copy in copies[2]:
        copy.wait()
    dy = jnp.concatenate([x_refs[j][1] for j in range(rows)], axis=0)
    size = FF // 3
    for f in range(3):
        cols = slice(size * f, size * (f + 1))
        up_cols = slice(FF + size * f, FF + size * (f + 1))
        gate = gu_ref[:, cols]
        up = gu_ref[:, up_cols]
        below = 0.5 + 0.5 * lax.erf(gate * math.sqrt(0.5))
        active = gate * below
        mid_ref[:, cols] = (active * up).astype(BF16)
        slope = below + gate * jnp.exp(-0.5 * gate * gate) * (1.0 / math.sqrt(2.0 * math.pi))
        dmid = dot(dy, w_down[cols, :], NT)
        dgu_ref[:, cols] = (dmid * up * slope).astype(BF16)
        dgu_ref[:, up_cols] = (dmid * active).astype(BF16)
    mixed = dot(mid_ref[...], w_down[...], NN)
    for j in range(rows):
        part = slice(tok * j, tok * (j + 1))
        out_refs[j][...] = (h_ref[part, :] + mixed[part, :]).astype(BF16)
    grad_normed = dot(dgu_ref[:, :D], w_in[0], NT)
    for t in range(1, 3):
        grad_normed = grad_normed + dot(dgu_ref[:, D * t : D * (t + 1)], w_in[t], NT)
    unit, inv_std = layer_norm(h_ref[...])
    gain_grad_ref[...] = jnp.broadcast_to(
        jnp.sum(grad_normed * unit, axis=0, keepdims=True), (8, D)
    )
    grad_hidden = dy.astype(F32) + norm_backward(grad_normed, unit, inv_std, gain)
    dh_ref[...] = grad_hidden
    branch_grad = grad_hidden.astype(BF16)
    do_ref[...] = dot(branch_grad, w_out[...], NT).astype(BF16)
    g_out[...] = dot(low_ref[...], branch_grad, TN).astype(BF16)
    for t in range(3):
        g_in[t] = dot(n_ref[...], dgu_ref[:, D * t : D * (t + 1)], TN).astype(BF16)
    g_down[...] = dot(mid_ref[...], dy, TN).astype(BF16)
    r, rf = block_size(plan)
    done = []
    for i in range(count):
        block = block_of(plan, meta, i)
        target = grads[i // plan.chips].at[i % plan.chips] if plan.aligned else grads[0]
        at = rows_at(block, r)
        done.append(
            pltpu.make_async_copy(g_out.at[at], target.at[pl.ds(0, r)], out_sems.at[5 * i])
        )
        for t in range(3):
            done.append(
                pltpu.make_async_copy(
                    g_in.at[t, at], target.at[pl.ds((1 + t) * r, r)], out_sems.at[5 * i + 1 + t]
                )
            )
        done.append(
            pltpu.make_async_copy(
                g_down.at[rows_at(block, rf)], target.at[pl.ds(4 * r, rf)], out_sems.at[5 * i + 4]
            )
        )
    for copy in done:
        copy.start()
    for copy in done:
        copy.wait()


def middle(plan, meta, low, gains, pieces, sources):
    local, rows, tok = plan.local, plan.rows, plan.tok
    count = len(sources)
    total = 4 * D + FF
    if plan.aligned:
        grads = [shape_of((plan.chips, plan.packed, D), BF16)] * 2
    else:
        grads = [shape_of((total, D), BF16)]
    return pl.pallas_call(
        functools.partial(middle_kernel, plan),
        in_specs=[SMEM, VMEM, VMEM] + [VMEM] * rows + [ANY] * count,
        out_specs=[VMEM] * (rows + 3) + [ANY] * len(grads),
        out_shape=[shape_of((tok, D), BF16)] * rows
        + [shape_of((local, D), BF16), shape_of((local, D), F32), shape_of((8, D), F32)]
        + grads,
        scratch_shapes=[
            pltpu.VMEM((D, D), BF16),
            pltpu.VMEM((3, D, D), BF16),
            pltpu.VMEM((FF, D), BF16),
            pltpu.VMEM((local, D), F32),
            pltpu.VMEM((local, D), BF16),
            pltpu.VMEM((local, 2 * FF), F32),
            pltpu.VMEM((local, FF), BF16),
            pltpu.VMEM((local, 2 * FF), BF16),
            pltpu.VMEM((D, D), BF16),
            pltpu.VMEM((3, D, D), BF16),
            pltpu.VMEM((FF, D), BF16),
            pltpu.SemaphoreType.DMA((5 * count,)),
            pltpu.SemaphoreType.DMA((5 * count,)),
        ],
        compiler_params=params(),
        cost_estimate=cost(6 * local * D * total, 4 * total * D + 12 * local * D),
        name="middle",
    )(meta, low, gains, *pieces, *sources)


def back_kernel(plan, meta, cos_ref, sin_ref, dq_ref, n_ref, dh_ref, gain_ref, g2_ref, *refs):
    rows, tok, groups = plan.rows, plan.tok, plan.groups
    count = source_count(plan)
    dkv = refs[:groups]
    x_refs = refs[groups : groups + rows]
    sources = refs[groups + rows : groups + rows + count]
    refs = refs[groups + rows + count :]
    in_refs = refs[:rows]
    grads = refs[rows : rows + (2 if plan.aligned else 1)]
    w_ref, dp_ref, g_ref, in_sems, out_sems = refs[rows + len(grads) :]
    copies = qkv_copies(plan, meta, sources, w_ref, in_sems)
    for copy in copies:
        copy.start()
    grad_keys = dkv[0][0].astype(F32)
    grad_values = dkv[0][1].astype(F32)
    for e in range(1, groups):
        grad_keys = grad_keys + dkv[e][0].astype(F32)
        grad_values = grad_values + dkv[e][1].astype(F32)
    dp_ref[0] = dq_ref[...]
    dp_ref[1] = rotate_all(grad_keys, cos_ref[...], sin_ref[...], -1.0).astype(BF16)
    dp_ref[2] = grad_values.astype(BF16)
    for t in range(3):
        g_ref[:, D * t : D * (t + 1)] = dot(n_ref[...], dp_ref[t], TN).astype(BF16)
    for copy in copies:
        copy.wait()
    grad_normed = dot(dp_ref[0], w_ref[:, :D], NT)
    for t in range(1, 3):
        grad_normed = grad_normed + dot(dp_ref[t], w_ref[:, D * t : D * (t + 1)], NT)
    gain_grad = jnp.zeros((1, D), F32)
    for j in range(rows):
        part = slice(tok * j, tok * (j + 1))
        unit, inv_std = layer_norm(x_refs[j][0].astype(F32))
        grad = grad_normed[part, :]
        gain_grad = gain_grad + jnp.sum(grad * unit, axis=0, keepdims=True)
        back = norm_backward(grad, unit, inv_std, gain_ref[0:1, :])
        in_refs[j][...] = (dh_ref[part, :] + back).astype(BF16)
    which = lax.broadcasted_iota(jnp.int32, (128, D), 0)
    both = jnp.where(which == 0, gain_grad, jnp.where(which == 1, g2_ref[0:1, :], 0.0))
    g_ref[:, 3 * D :] = both.T.astype(BF16)
    r, _ = block_size(plan)
    done = []
    for i in range(count):
        target = grads[i // plan.chips].at[i % plan.chips] if plan.aligned else grads[0]
        at = rows_at(block_of(plan, meta, i), r)
        done.append(pltpu.make_async_copy(g_ref.at[at], target, out_sems.at[i]))
    for copy in done:
        copy.start()
    for copy in done:
        copy.wait()


def back(plan, meta, cosine, sine, dq, normed, dhidden, gains, gain_two, dkv, pieces, sources):
    local, rows, tok = plan.local, plan.rows, plan.tok
    count = len(sources)
    if plan.aligned:
        grads = [shape_of((plan.chips, plan.r, EXT), BF16)] * 2
    else:
        grads = [shape_of((D, EXT), BF16)]
    return pl.pallas_call(
        functools.partial(back_kernel, plan),
        in_specs=[SMEM] + [VMEM] * (7 + plan.groups + rows) + [ANY] * count,
        out_specs=[VMEM] * rows + [ANY] * len(grads),
        out_shape=[shape_of((tok, D), BF16)] * rows + grads,
        scratch_shapes=[
            pltpu.VMEM((D, EXT), BF16),
            pltpu.VMEM((3, local, D), BF16),
            pltpu.VMEM((D, EXT), BF16),
            pltpu.SemaphoreType.DMA((count,)),
            pltpu.SemaphoreType.DMA((count,)),
        ],
        compiler_params=params(),
        cost_estimate=cost(4 * local * D * 3 * D, 4 * D * EXT + 20 * local * D),
        name="back",
    )(meta, cosine, sine, dq, normed, dhidden, gains, gain_two, *dkv, *pieces, *sources)


def pad_width(plan):
    return -(-(3 * plan.cw + 2) // 128) * 128


def cut_qkv_kernel(plan, meta, total, *refs):
    outs, held = refs[: plan.nrow], refs[plan.nrow]
    width, wide = 3 * plan.cw, pad_width(plan)
    for z in range(plan.nrow):
        place_at = meta[plan.at_z + z]
        held[place_at, :, :width] = total[:, width * z : width * (z + 1)]
        held[place_at, :, width:] = total[:, 3 * D : 3 * D + wide - width]
    for j in range(plan.nrow):
        outs[j][...] = held[j]


def cut_qkv(plan, meta, total):
    width, wide = 3 * plan.cw, pad_width(plan)
    if not plan.aligned:
        parts = [
            jnp.concatenate(
                [total[:, width * z : width * (z + 1)], total[:, 3 * D : 3 * D + wide - width]],
                axis=1,
            )
            for z in range(plan.nrow)
        ]
        return ordered(plan, meta, parts)
    return pl.pallas_call(
        functools.partial(cut_qkv_kernel, plan),
        in_specs=[SMEM, VMEM],
        out_specs=[VMEM] * plan.nrow,
        out_shape=[shape_of((plan.r, wide), BF16)] * plan.nrow,
        scratch_shapes=[pltpu.VMEM((plan.nrow, plan.r, wide), BF16)],
        compiler_params=params(),
        cost_estimate=cost(0, 4 * plan.r * EXT),
        name="cut_qkv",
    )(meta, total)


def cut_rest_kernel(plan, meta, total, *refs):
    outs, held = refs[: plan.nrow], refs[plan.nrow]
    r, rf, cw = plan.r, plan.rf, plan.cw
    for z in range(plan.nrow):
        place_at = meta[plan.at_z + z]
        cols = slice(cw * z, cw * (z + 1))
        parts = []
        for i in range(3):
            block, at = (3 * z + i) // plan.nrow, (3 * z + i) % plan.nrow
            parts.append(total[r * (1 + block) : r * (2 + block), cw * at : cw * (at + 1)])
        held[place_at, :r, :] = jnp.concatenate([parts[0], parts[2]], axis=1)
        held[place_at, r : 2 * r, :] = jnp.concatenate(
            [parts[1], total[4 * r : 5 * r, cols]], axis=1
        )
        rest = total[5 * r : 4 * r + rf, cols]
        blank = jnp.zeros((2 * r - rf, cw), BF16)
        held[place_at, 2 * r :, :] = jnp.concatenate(
            [total[:r, cols], jnp.concatenate([rest, blank], axis=0)], axis=1
        )
    for j in range(plan.nrow):
        outs[j][...] = held[j]


def cut_rest(plan, meta, total):
    r, cw = plan.r, plan.cw
    if not plan.aligned:
        grad_in = jnp.concatenate([total[r * (1 + t) : r * (2 + t)] for t in range(3)], axis=1)
        parts = [
            pack_rest(
                plan,
                total[:r, cw * z : cw * (z + 1)],
                grad_in[:, 3 * cw * z : 3 * cw * (z + 1)],
                total[4 * r :, cw * z : cw * (z + 1)],
            )
            for z in range(plan.nrow)
        ]
        return ordered(plan, meta, parts)
    return pl.pallas_call(
        functools.partial(cut_rest_kernel, plan),
        in_specs=[SMEM, VMEM],
        out_specs=[VMEM] * plan.nrow,
        out_shape=[shape_of((3 * r, 2 * cw), BF16)] * plan.nrow,
        scratch_shapes=[pltpu.VMEM((plan.nrow, 3 * r, 2 * cw), BF16)],
        compiler_params=params(),
        cost_estimate=cost(0, 4 * plan.packed * D),
        name="cut_rest",
    )(meta, total)


def reduce_z(plan, pieces):
    return [pieces[0]] + [
        lax.ppermute(pieces[j], "row", plan.z_pairs(j)) for j in range(1, plan.nrow)
    ]


def sum_pieces(pieces):
    total = pieces[0].astype(F32)
    for piece in pieces[1:]:
        total = total + piece.astype(F32)
    return total


def end_rest_kernel(plan, *refs):
    pieces, (g_out, g_in, g_down) = refs[: plan.nrow], refs[plan.nrow :]
    total = sum_pieces([piece[...] for piece in pieces])
    parts_in, part_out, part_down = unpack_rest(plan, total)
    g_out[...] = part_out
    g_in[...] = jnp.concatenate(parts_in, axis=1)
    g_down[...] = part_down


def end_rest(plan, pieces):
    if not plan.aligned:
        parts_in, part_out, part_down = unpack_rest(plan, sum_pieces(pieces))
        return part_out, jnp.concatenate(parts_in, axis=1), part_down
    return pl.pallas_call(
        functools.partial(end_rest_kernel, plan),
        in_specs=[VMEM] * plan.nrow,
        out_specs=[VMEM] * 3,
        out_shape=[
            shape_of((plan.r, plan.cw), F32),
            shape_of((plan.r, 3 * plan.cw), F32),
            shape_of((plan.rf, plan.cw), F32),
        ],
        compiler_params=params(),
        cost_estimate=cost(0, 6 * plan.packed * D),
        name="end_rest",
    )(*pieces)


def end_qkv_kernel(plan, *refs):
    pieces, (g_qkv, g_gain) = refs[: plan.nrow], refs[plan.nrow :]
    width, wide = 3 * plan.cw, pad_width(plan)
    total = sum_pieces([piece[...] for piece in pieces])
    g_qkv[...] = total[:, :width]
    tail = total[:, wide - 128 :]
    g_gain[...] = tail.T


def end_qkv(plan, pieces):
    width, wide = 3 * plan.cw, pad_width(plan)
    if not plan.aligned:
        total = sum_pieces(pieces)
        return total[:, :width], total[:, width], total[:, width + 1]
    grad, gain = pl.pallas_call(
        functools.partial(end_qkv_kernel, plan),
        in_specs=[VMEM] * plan.nrow,
        out_specs=[VMEM] * 2,
        out_shape=[shape_of((plan.r, width), F32), shape_of((128, plan.r), F32)],
        compiler_params=params(),
        cost_estimate=cost(0, 6 * plan.r * EXT),
        name="end_qkv",
    )(*pieces)
    at = width - (wide - 128)
    return grad, gain[at], gain[at + 1]


def rotation_tables(plan, meta, lengths):
    ends = jnp.cumsum(lax.dynamic_index_in_dim(lengths, meta[plan.at_lo], 0, keepdims=False))
    starts = jnp.concatenate([jnp.zeros((1,), jnp.int32), ends[:-1]])
    bases = meta[plan.at_base : plan.at_base + plan.rows]
    places = (bases[:, None] + jnp.arange(plan.tok, dtype=jnp.int32)[None, :]).reshape(-1)
    passed = places[:, None] >= starts[None, :]
    positions = places - jnp.max(jnp.where(passed, starts[None, :], 0), axis=1)
    half = HD // 2
    inverse = ROPE_BASE ** (-(jnp.arange(half, dtype=F32) * (2.0 / HD)))
    angles = positions.astype(F32)[:, None] * inverse
    cosine, sine = jnp.cos(angles), jnp.sin(angles)
    return (
        jnp.concatenate([cosine] * 4, axis=1),
        jnp.concatenate([-sine, sine, -sine, sine], axis=1),
    )


def body(
    plan,
    tokens,
    lengths,
    norm_gain,
    qkv_weight,
    out_weight,
    mlp_gain,
    in_weight,
    down_weight,
    cotangent,
):
    blk, row = lax.axis_index("blk"), lax.axis_index("row")
    meta = lax.dynamic_slice(
        jnp.asarray(plan.table), (row, blk, 0), (1, 1, plan.size)
    ).reshape(plan.size)
    qkv_parts = gather_z(plan, qkv_weight)
    pieces = exchange_rows(plan, pick(plan, meta, tokens, cotangent))
    rest_parts = gather_z(plan, pack_rest(plan, out_weight, in_weight, down_weight))
    gains = jnp.pad(jnp.stack([norm_gain, mlp_gain], axis=1), ((0, 0), (0, 126)))
    cosine, sine = rotation_tables(plan, meta, lengths)
    qkv_own, qkv_other = gather_xy(plan, join_qkv(plan, meta, gains, qkv_parts))
    qkv_from = qkv_sources(plan, meta, qkv_own, qkv_other)
    queries, kv, normed, gains = project(plan, meta, cosine, sine, pieces, qkv_from)
    kv_all = [kv] + [
        lax.ppermute(kv, "blk", plan.xor_pairs(plan.member(e))) for e in range(1, plan.groups)
    ]
    rest_own, rest_other = gather_xy(plan, join_rest(plan, meta, rest_parts))
    rest_from = rest_sources(plan, meta, rest_own, rest_other)
    heads, low, lse = attend(plan, meta, lengths, queries, kv_all)
    results = middle(plan, meta, low, gains, pieces, rest_from)
    outs, (dout, dhidden, gain_two) = results[: plan.rows], results[plan.rows : plan.rows + 3]
    rest_grads = results[plan.rows + 3 :]
    if not plan.aligned:
        r, rf, nblk = plan.r, plan.rf, plan.nblk
        whole = rest_grads[0]
        blocks = [whole[D * i : D * (i + 1)].reshape(nblk, r, D) for i in range(4)]
        blocks.append(whole[4 * D :].reshape(nblk, rf, D))
        rest_grads = split_blocks(plan, meta, jnp.concatenate(blocks, axis=1))
    output = place(plan, meta, exchange_rows(plan, outs))
    rest_sum = reduce_xy(plan, *rest_grads)
    back_results = attend_back(
        plan, meta, lengths, queries, dout, heads, lse, cosine, sine, kv_all
    )
    dq, dkv = back_results[0], list(back_results[1:])
    for e in range(1, plan.groups):
        dkv[e] = lax.ppermute(dkv[e], "blk", plan.xor_pairs(plan.member(e)))
    rest_pieces = reduce_z(plan, cut_rest(plan, meta, rest_sum))
    out_grad, in_grad, down_grad = end_rest(plan, rest_pieces)
    results = back(
        plan, meta, cosine, sine, dq, normed, dhidden, gains, gain_two, dkv, pieces, qkv_from
    )
    qkv_grads = results[plan.rows :]
    if not plan.aligned:
        qkv_grads = split_blocks(plan, meta, qkv_grads[0].reshape(plan.nblk, plan.r, EXT))
    qkv_sum = reduce_xy(plan, *qkv_grads)
    input_grad = place(plan, meta, exchange_rows(plan, results[: plan.rows]))
    qkv_pieces = reduce_z(plan, cut_qkv(plan, meta, qkv_sum))
    qkv_grad, norm_gain_grad, mlp_gain_grad = end_qkv(plan, qkv_pieces)
    return (
        output,
        input_grad,
        norm_gain_grad,
        qkv_grad,
        out_grad,
        mlp_gain_grad,
        in_grad,
        down_grad,
    )


def solution(mesh):
    weights = P("blk", "row")
    acts = P("row", "blk", None)

    def run(*args):
        rows = args[0].shape[0] // mesh.shape["row"]
        tok = args[0].shape[1] // mesh.shape["blk"]
        plan = Plan(mesh, rows, tok)
        return jax.shard_map(
            functools.partial(body, plan),
            mesh=mesh,
            in_specs=(acts, P("row", None), P("blk"), weights, weights, P("blk"), weights, weights, acts),
            out_specs=(acts, acts, P("blk"), weights, weights, P("blk"), weights, weights),
            check_vma=False,
        )(*args)

    return run
```

time: 891 us -> 370 us (0.42); the launches traced: 875 us -> 368 us
  local copies, waits for them, and re-layouts: 267 us -> 17.1 us
  Pallas kernels: 0 us -> 193 us
  matrix products: 162 us -> 0 us
  blocking collectives: 152 us -> 0 us
  loops' own time: 62.4 us -> 0 us
  other arithmetic: 65.9 us -> 8.16 us
  waiting for transfers between devices: 149 us -> 92.2 us
  starting transfers between devices: 1.13 us -> 55 us
  between operations: 16.5 us -> 3.16 us
    pallas_call x0 -> x14, Pallas kernels: none -> 193 us  [the longest x2 51.2 us: place(): pl.pallas_call(functools.partial(place_kernel, plan), in_specs=[SMEM] + [...]
    dot_general x54 -> x0, matrix products: 162 us -> none  [the longest x6 28.1 us: key_accumulate(): jnp.einsum('hqk,qhd->khd', dscores, row_bq, preferred_element_type=jnp.fl...]
    reduce_scatter x4 -> x0, waiting for transfers between devices: 95.2 us -> none  [the longest x1 39.2 us: body(): lax.psum_scatter(grad_down.astype(jnp.bfloat16), 'blk', scatter_dimension...]
    all_gather x6 -> x0, blocking collectives: 93.6 us -> none  [the longest x1 23.7 us: body(): lax.all_gather(delta.astype(jnp.bfloat16), 'blk', axis=2, tiled=True)]
    ppermute x0 -> x45, waiting for transfers between devices: none -> 92.2 us  [the longest x4 29.9 us: reduce_xy(): moved = lax.ppermute(high, 'blk', plan.step_pairs(step))]
    dynamic_slice x60 -> x1, local copies, waits for them, and re-layouts: 78.1 us -> 0.69 us  [body(): lax.dynamic_slice(jnp.asarray(plan.table), (row, blk, 0), (1, 1, plan.size))]
    another operation x33 -> x0, loops' own time: 62.4 us -> none  [the longest x2 21.1 us: key_grads(): lax.map(key_per_row, (state, block_queries, block_dout, block_lse, block_...]
    squeeze x44 -> x1, local copies, waits for them, and re-layouts: 58.7 us -> 1.28 us  [end_qkv(): return (grad, gain[at], gain[at + 1])]
  transfers between devices with their start and end apart: 16 -> 45, of which waited for: 6 -> 16; matrix products, arithmetic and copies ran while one was open for 53% -> 4% of each run, Pallas kernels for 0% -> 36%
where the time goes in v1:
time: 370 us; the launch traced here: 368 us
  Pallas kernels  193 us (52%)
  waiting for transfers between devices  92.2 us (25%)
  starting transfers between devices  55 us (15%)
  local copies, waits for them, and re-layouts  17.1 us (5%)
  other arithmetic  8.16 us (2%)
    pallas_call x2, Pallas kernels, place(): pl.pallas_call(functools.partial(place_kernel, plan), in_specs=[SMEM] + [...  51.2 us
    pallas_call x1, Pallas kernels, pick(): pl.pallas_call(functools.partial(pick_kernel, plan), in_specs=[SMEM, ANY,...  49.5 us
    ppermute x4, waiting for transfers between devices, reduce_xy(): moved = lax.ppermute(high, 'blk', plan.step_pairs(step))  29.9 us
    ppermute x6, waiting for transfers between devices, gather_xy(): more = [lax.ppermute(piece, 'blk', pairs) for piece in pieces]  27.7 us
    pallas_call x1, Pallas kernels, attend_back(): pl.pallas_call(functools.partial(attend_back_kernel, plan, width), grid=(...  21.8 us
    pallas_call x1, Pallas kernels, middle(): pl.pallas_call(functools.partial(middle_kernel, plan), in_specs=[SMEM, VM...  21.1 us
    ppermute x6, starting transfers between devices, reduce_z(): lax.ppermute(pieces[j], 'row', plan.z_pairs(j))  16.7 us
    pallas_call x1, Pallas kernels, attend(): pl.pallas_call(functools.partial(attend_kernel, plan, width), grid=(PAIRS...  16.4 us
  transfers between devices with their start and end apart: 45, of which 16 were waited for; matrix products, arithmetic and copies ran while one was open for 4% of the time, Pallas kernels for 36%

profile of v1, /device:TPU:0, one launch (start us, length us, event | category | flops | bytes accessed | tf_op | source)
XLA Modules:
  0.0 368.4 jit_solution(15337721278288205529)
XLA Ops:
  0.6 4.1 %collective-permute-start.4 = (bf16[96,576]{1,0:T(8,128)(2,1)}, bf16[96,576]{1,0:T(8,128)(2,1)S(1)}, u32[]{:S(2)}, u32[]{:S(2)}) collective-permute-start(bf16[96,576]{1,0:T(8,128)(2,1)} %refs_0_.1), channel_id=1, source_target_pairs={{0,16},{8,24},{16,0},{24,8},{1,17},{9,25},{17,1},{25,9},{2,18},{10... | collective-permute-start | bytes 331784 | tf_op jit(solution)/shard_map/ppermute | solution.py:120
  4.7 1.6 collective-permute-start.3
  8.4 3.9 %collective-permute-start.16 = (bf16[288,384]{1,0:T(8,128)(2,1)S(1)}, bf16[288,384]{1,0:T(8,128)(2,1)S(1)}, u32[]{:S(2)}, u32[]{:S(2)}) collective-permute-start(bf16[288,384]{1,0:T(8,128)(2,1)S(1)} %maximum_maximum_fusion.refs_0_), channel_id=1, source_target_pairs={{0,24},{8,16},{16,8},{24,0},{1,25},{9,17},{17,9},{25,1},{2,26},{10... | collective-permute-start | bytes 663560 | tf_op jit(solution)/shard_map/ppermute | solution.py:120
  16.9 1.2 fusion.6.meta
  20.1 2.1 join_qkv.1.refs_4_.refs_6_
  22.2 5.9 %collective-permute-start.6 = (bf16[96,2432]{1,0:T(8,128)(2,1)}, bf16[96,2432]{1,0:T(8,128)(2,1)S(1)}, u32[]{:S(2)}, u32[]{:S(2)}) collective-permute-start(bf16[96,2432]{1,0:T(8,128)(2,1)} %join_qkv.1.refs_4_.refs_6_), channel_id=1, source_target_pairs={{0,2},{1,5},{2,0},{3,7},{4,6},{5,1},{6,4},{7,3},{8,10},{9,13},{10,... | collective-permute-start | bytes 1400840 | tf_op jit(solution)/shard_map/ppermute | solution.py:134
  29.1 1.5 collective-permute-start.7
  30.6 9.3 %collective-permute-done.6.refs_5_.refs_7_ = bf16[96,2432]{1,0:T(8,128)(2,1)S(1)} collective-permute-done((bf16[96,2432]{1,0:T(8,128)(2,1)}, bf16[96,2432]{1,0:T(8,128)(2,1)S(1)}, u32[]{:S(2)}, u32[]{:S(2)}) %collective-permute-start.6) | collective-permute-done | bytes 466976 | tf_op jit(solution)/shard_map/ppermute | solution.py:134
  41.1 49.5 %pick_rows.1 = (bf16[2,128,768]{2,1,0:T(8,128)(2,1)}, bf16[2,128,768]{2,1,0:T(8,128)(2,1)}, bf16[2,128,768]{2,1,0:T(8,128)(2,1)}, bf16[2,128,768]{2,1,0:T(8,128)(2,1)}) custom-call(s32[25]{0:T(128)} %fusion.6.meta, bf16[4,128,768]{2,1,0:T(8,128)(2,1)} %tokens.1, bf16[4,128,768]{2,1,0:T(8,128)(2,1)} %cotangent.1), custom_call_target="tpu_custom_call" | custom-call | bytes 3145728 | tf_op jit(solution)/shard_map/pick_rows/pallas_call | solution.py:210
  90.6 1.6 collective-permute-start
  94.5 4.2 %collective-permute-done.refs_1_.refs_3_ = bf16[2,128,768]{2,1,0:T(8,128)(2,1)S(1)} collective-permute-done((bf16[2,128,768]{2,1,0:T(8,128)(2,1)}, bf16[2,128,768]{2,1,0:T(8,128)(2,1)S(1)}, u32[]{:S(2)}, u32[]{:S(2)}) %collective-permute-start) | collective-permute-done | bytes 393248 | tf_op jit(solution)/shard_map/ppermute | solution.py:125
  98.6 5.7 %collective-permute-done.1.refs_2_.refs_4_ = bf16[2,128,768]{2,1,0:T(8,128)(2,1)S(1)} collective-permute-done((bf16[2,128,768]{2,1,0:T(8,128)(2,1)}, bf16[2,128,768]{2,1,0:T(8,128)(2,1)S(1)}, u32[]{:S(2)}, u32[]{:S(2)}) %collective-permute-start.1) | collective-permute-done | bytes 393248 | tf_op jit(solution)/shard_map/ppermute | solution.py:125
  106.0 2.5 join_rest.1.refs_4_
  108.6 1.3 pad_maximum_fusion
  111.2 7.3 %project.1 = (bf16[512,768]{1,0:T(8,128)(2,1)}, bf16[2,512,768]{2,1,0:T(8,128)(2,1)}, bf16[512,768]{1,0:T(8,128)(2,1)}, f32[8,768]{1,0:T(8,128)}) custom-call(s32[25]{0:T(128)} %fusion.6.meta, f32[512,128]{1,0:T(8,128)} %get-tuple-element.108.cos_ref, f32[512,128]{1,0:T(8,128)} %get-tuple-element.109.sin_ref, ...), custom_call_target="tpu_custom_call" | custom-call | flops 1811939328 | bytes 8454144 | tf_op jit(solution)/shard_map/project/pallas_call | solution.py:431
  118.5 1.4 collective-permute-start.13
  122.8 9.3 %collective-permute-done.18.refs_6_ = bf16[528,768]{1,0:T(8,128)(2,1)S(1)} collective-permute-done((bf16[528,768]{1,0:T(8,128)(2,1)S(1)}, bf16[528,768]{1,0:T(8,128)(2,1)S(1)}, u32[]{:S(2)}, u32[]{:S(2)}) %collective-permute-start.18) | collective-permute-done | bytes 811040 | tf_op jit(solution)/shard_map/ppermute | solution.py:134
  132.1 8.7 %collective-permute-done.19.refs_7_ = bf16[528,768]{1,0:T(8,128)(2,1)S(1)} collective-permute-done((bf16[528,768]{1,0:T(8,128)(2,1)S(1)}, bf16[528,768]{1,0:T(8,128)(2,1)S(1)}, u32[]{:S(2)}, u32[]{:S(2)}) %collective-permute-start.19) | collective-permute-done | bytes 811040 | tf_op jit(solution)/shard_map/ppermute | solution.py:134
  142.0 16.4 %attend.1 = (f32[512,768]{1,0:T(8,128)}, bf16[512,768]{1,0:T(8,128)(2,1)}, f32[6,2,512]{2,1,0:T(2,128)}) custom-call(s32[25]{0:T(128)} %fusion.6.meta, s32[4,8]{1,0:T(4,128)} %lengths.3, bf16[512,768]{1,0:T(8,128)(2,1)} %get-tuple-element.54.q_ref, bf16[2,512,768]{2,1,0:T(8,128)(2,1)} %get-tuple-element.55.refs_0_, bf16[2,512,768]{2,1,0:T(8,128)(2,1)} %copy-done.23), custom_call_target="tpu_custom_call" | custom-call | flops 6442450944 | bytes 6291456 | tf_op jit(solution)/shard_map/attend/pallas_call | solution.py:529
  160.1 21.1 %middle.1 = (bf16[128,768]{1,0:T(8,128)(2,1)}, bf16[128,768]{1,0:T(8,128)(2,1)}, bf16[128,768]{1,0:T(8,128)(2,1)}, bf16[128,768]{1,0:T(8,128)(2,1)}, bf16[512,76...) custom-call(s32[25]{0:T(128)} %fusion.6.meta, ...), custom_call_target="tpu_custom_call" | custom-call | flops 9965666304 | bytes 17694720 | tf_op jit(solution)/shard_map/middle/pallas_call | solution.py:744
  181.2 21.8 %attend_back.1 = (bf16[512,768]{1,0:T(8,128)(2,1)}, bf16[2,512,768]{2,1,0:T(8,128)(2,1)}, bf16[2,512,768]{2,1,0:T(8,128)(2,1)}) custom-call(s32[25]{0:T(128)} %fusion.6.meta, s32[4,8]{1,0:T(4,128)} %lengths.3, bf16[512,768]{1,0:T(8,128)(2,1)} %get-tuple-element.54.q_ref, bf16[512,768]{1,0:T(8,128)(2,1)} %get-tuple-element.62.do_ref, ...), custom_call_target="tpu_custom_call" | custom-call | flops 16106127360 | bytes 11010048 | tf_op jit(solution)/shard_map/attend_back/pallas_call | solution.py:607
  203.5 3.2 collective-permute-done.27.refs_1_
  207.9 12.7 %back.1 = (bf16[128,768]{1,0:T(8,128)(2,1)}, bf16[128,768]{1,0:T(8,128)(2,1)}, bf16[128,768]{1,0:T(8,128)(2,1)}, bf16[128,768]{1,0:T(8,128)(2,1)}, bf16[4,96,243...) custom-call(s32[25]{0:T(128)} %fusion.6.meta, f32[512,128]{1,0:T(8,128)} %get-tuple-element.108.cos_ref, ...), custom_call_target="tpu_custom_call" | custom-call | flops 3623878656 | bytes 15335424 | tf_op jit(solution)/shard_map/back/pallas_call | solution.py:830
  220.6 1.7 fusion.4
  225.0 1.3 collective-permute-done.32
  228.6 2.3 collective-permute-done.39
  232.6 7.8 %collective-permute-done.33 = bf16[2,96,2432]{2,1,0:T(8,128)(2,1)S(1)} collective-permute-done((bf16[2,96,2432]{2,1,0:T(8,128)(2,1)S(1)}, bf16[2,96,2432]{2,1,0:T(8,128)(2,1)S(1)}, u32[]{:S(2)}, u32[]{:S(2)}) %collective-permute-start.33) | collective-permute-done | bytes 933920 | tf_op jit(solution)/shard_map/ppermute | solution.py:151
  241.3 1.3 collective-permute-start.24
  243.4 1.4 collective-permute-start.26
  244.8 22.2 %collective-permute-done.40 = bf16[2,528,768]{2,1,0:T(8,128)(2,1)S(1)} collective-permute-done((bf16[2,528,768]{2,1,0:T(8,128)(2,1)S(1)}, bf16[2,528,768]{2,1,0:T(8,128)(2,1)S(1)}, u32[]{:S(2)}, u32[]{:S(2)}) %collective-permute-start.40) | collective-permute-done | bytes 1622048 | tf_op jit(solution)/shard_map/ppermute | solution.py:151
  268.0 1.3 collective-permute-start.29
  269.2 2.0 collective-permute-done.25.refs_2_
  271.2 1.4 collective-permute-start.30
  273.6 2.0 cut_qkv.1
  275.6 7.6 %collective-permute-start.35 = (bf16[96,640]{1,0:T(8,128)(2,1)}, bf16[96,640]{1,0:T(8,128)(2,1)S(1)}, u32[]{:S(2)}, u32[]{:S(2)}) collective-permute-start(bf16[96,640]{1,0:T(8,128)(2,1)} %get-tuple-element.78), channel_id=1, source_target_pairs={{0,8},{8,0},{16,24},{24,16},{1,9},{9,1},{17,25},{25,17},{2,10},{10... | collective-permute-start | bytes 368648 | tf_op jit(solution)/shard_map/ppermute | solution.py:937
  283.2 2.7 collective-permute-start.36
  286.0 1.5 collective-permute-start.37
  287.4 25.6 %place_rows.2 = bf16[4,128,768]{2,1,0:T(8,128)(2,1)} custom-call(s32[25]{0:T(128)} %fusion.6.meta, bf16[128,768]{1,0:T(8,128)(2,1)} %get-tuple-element.58.refs_0_, bf16[128,768]{1,0:T(8,128)(2,1)} %copy-done.11, bf16[128,768]{1,0:T(8,128)(2,1)} %copy-done.12, bf16[128,768]{1,0:T(8,128)(2,1)} %copy-done.13), custom_call_target="tpu_custom_call" | custom-call | bytes 1572864 | tf_op jit(solution)/shard_map/place_rows/pallas_call | solution.py:235
  313.8 25.6 %place_rows.3 = bf16[4,128,768]{2,1,0:T(8,128)(2,1)} custom-call(s32[25]{0:T(128)} %fusion.6.meta, bf16[128,768]{1,0:T(8,128)(2,1)} %get-tuple-element.71.refs_0_, bf16[128,768]{1,0:T(8,128)(2,1)} %copy-done.14, bf16[128,768]{1,0:T(8,128)(2,1)} %copy-done.15, bf16[128,768]{1,0:T(8,128)(2,1)} %copy-done.16), custom_call_target="tpu_custom_call" | custom-call | bytes 1572864 | tf_op jit(solution)/shard_map/place_rows/pallas_call | solution.py:235
  340.1 1.9 end_qkv.1
  342.0 1.2 fusion.total
  343.2 2.3 cut_rest.1
  345.5 2.5 collective-permute-start.42
  348.5 2.0 collective-permute-start.44
  350.4 1.3 slice_bitcast_fusion
  351.7 2.7 collective-permute-done.42.refs_1_
  354.4 11.1 %collective-permute-done.43.refs_2_ = bf16[288,384]{1,0:T(8,128)(2,1)S(1)} collective-permute-done((bf16[288,384]{1,0:T(8,128)(2,1)}, bf16[288,384]{1,0:T(8,128)(2,1)S(1)}, u32[]{:S(2)}, u32[]{:S(2)}) %collective-permute-start.43) | collective-permute-done | bytes 221216 | tf_op jit(solution)/shard_map/ppermute | solution.py:937
  366.2 2.1 end_rest.1
  (181 shorter events, 34.4 us)
Async XLA Ops:
  0.6 17.5 %collective-permute-start.4 = (bf16[96,576]{1,0:T(8,128)(2,1)}, bf16[96,576]{1,0:T(8,128)(2,1)S(1)}, u32[]{:S(2)}, u32[]{:S(2)}) collective-permute-start(bf16[96,576]{1,0:T(8,128)(2,1)} %refs_0_.1), channel_id=1, source_target_pairs={{0,16},{8,24},{16,0},{24,8},{1,17},{9,25},{17,1},{25,9},{2,18},{10... | collective-permute-start | bytes 331784 | tf_op jit(solution)/shard_map/ppermute | solution.py:120
  4.7 14.1 %collective-permute-start.3 = (bf16[96,576]{1,0:T(8,128)(2,1)}, bf16[96,576]{1,0:T(8,128)(2,1)S(1)}, u32[]{:S(2)}, u32[]{:S(2)}) collective-permute-start(bf16[96,576]{1,0:T(8,128)(2,1)} %refs_0_.1), channel_id=1, source_target_pairs={{0,8},{8,0},{16,24},{24,16},{1,9},{9,1},{17,25},{25,17},{2,10},{10... | collective-permute-start | bytes 331784 | tf_op jit(solution)/shard_map/ppermute | solution.py:120
  6.3 12.5 %collective-permute-start.5 = (bf16[96,576]{1,0:T(8,128)(2,1)}, bf16[96,576]{1,0:T(8,128)(2,1)S(1)}, u32[]{:S(2)}, u32[]{:S(2)}) collective-permute-start(bf16[96,576]{1,0:T(8,128)(2,1)} %refs_0_.1), channel_id=1, source_target_pairs={{0,24},{8,16},{16,8},{24,0},{1,25},{9,17},{17,9},{25,1},{2,26},{10... | collective-permute-start | bytes 331784 | tf_op jit(solution)/shard_map/ppermute | solution.py:120
  8.4 97.6 %copy-start.3 = (bf16[288,384]{1,0:T(8,128)(2,1)}, bf16[288,384]{1,0:T(8,128)(2,1)S(1)}, u32[]{:S(2)}) copy-start(bf16[288,384]{1,0:T(8,128)(2,1)S(1)} %maximum_maximum_fusion.refs_0_) | copy-start | bytes 663556
  8.4 82.2 %collective-permute-start.16 = (bf16[288,384]{1,0:T(8,128)(2,1)S(1)}, bf16[288,384]{1,0:T(8,128)(2,1)S(1)}, u32[]{:S(2)}, u32[]{:S(2)}) collective-permute-start(bf16[288,384]{1,0:T(8,128)(2,1)S(1)} %maximum_maximum_fusion.refs_0_), channel_id=1, source_target_pairs={{0,24},{8,16},{16,8},{24,0},{1,25},{9,17},{17,9},{25,1},{2,26},{10... | collective-permute-start | bytes 663560 | tf_op jit(solution)/shard_map/ppermute | solution.py:120
  12.3 79.9 %collective-permute-start.15 = (bf16[288,384]{1,0:T(8,128)(2,1)S(1)}, bf16[288,384]{1,0:T(8,128)(2,1)S(1)}, u32[]{:S(2)}, u32[]{:S(2)}) collective-permute-start(bf16[288,384]{1,0:T(8,128)(2,1)S(1)} %maximum_maximum_fusion.refs_0_), channel_id=1, source_target_pairs={{0,16},{8,24},{16,0},{24,8},{1,17},{9,25},{17,1},{25,9},{2,18},{10... | collective-permute-start | bytes 663560 | tf_op jit(solution)/shard_map/ppermute | solution.py:120
  18.2 75.4 %collective-permute-start.14 = (bf16[288,384]{1,0:T(8,128)(2,1)S(1)}, bf16[288,384]{1,0:T(8,128)(2,1)S(1)}, u32[]{:S(2)}, u32[]{:S(2)}) collective-permute-start(bf16[288,384]{1,0:T(8,128)(2,1)S(1)} %maximum_maximum_fusion.refs_0_), channel_id=1, source_target_pairs={{0,8},{8,0},{16,24},{24,16},{1,9},{9,1},{17,25},{25,17},{2,10},{10... | collective-permute-start | bytes 663560 | tf_op jit(solution)/shard_map/ppermute | solution.py:120
  22.2 17.7 %collective-permute-start.6 = (bf16[96,2432]{1,0:T(8,128)(2,1)}, bf16[96,2432]{1,0:T(8,128)(2,1)S(1)}, u32[]{:S(2)}, u32[]{:S(2)}) collective-permute-start(bf16[96,2432]{1,0:T(8,128)(2,1)} %join_qkv.1.refs_4_.refs_6_), channel_id=1, source_target_pairs={{0,2},{1,5},{2,0},{3,7},{4,6},{5,1},{6,4},{7,3},{8,10},{9,13},{10,... | collective-permute-start | bytes 1400840 | tf_op jit(solution)/shard_map/ppermute | solution.py:134
  29.1 75.3 %collective-permute-start.7 = (bf16[96,2432]{1,0:T(8,128)(2,1)}, bf16[96,2432]{1,0:T(8,128)(2,1)S(1)}, u32[]{:S(2)}, u32[]{:S(2)}) collective-permute-start(bf16[96,2432]{1,0:T(8,128)(2,1)} %join_qkv.1.refs_4_.refs_6_), channel_id=1, source_target_pairs={{0,4},{1,3},{2,6},{3,1},{4,0},{5,7},{6,2},{7,5},{8,12},{9,11},{10,... | collective-permute-start | bytes 1400840 | tf_op jit(solution)/shard_map/ppermute | solution.py:134
  39.9 68.7 %copy-start.32 = (bf16[96,2432]{1,0:T(8,128)(2,1)}, bf16[96,2432]{1,0:T(8,128)(2,1)S(1)}, u32[]{:S(2)}) copy-start(bf16[96,2432]{1,0:T(8,128)(2,1)S(1)} %collective-permute-done.6.refs_5_.refs_7_) | copy-start | bytes 1400836
  39.9 65.0 %collective-permute-start.8 = (bf16[96,2432]{1,0:T(8,128)(2,1)S(1)}, bf16[96,2432]{1,0:T(8,128)(2,1)S(1)}, u32[]{:S(2)}, u32[]{:S(2)}) collective-permute-start(bf16[96,2432]{1,0:T(8,128)(2,1)S(1)} %collective-permute-done.6.refs_5_.refs_7_), channel_id=1, source_target_pairs={{0,4},{1,3},{2,6},{3,1},{4,0},{5,7},{6,2},{7,5},{8,12},{9,11},{10,... | collective-permute-start | bytes 1400840 | tf_op jit(solution)/shard_map/ppermute | solution.py:134
  90.6 8.1 %collective-permute-start = (bf16[2,128,768]{2,1,0:T(8,128)(2,1)}, bf16[2,128,768]{2,1,0:T(8,128)(2,1)S(1)}, u32[]{:S(2)}, u32[]{:S(2)}) collective-permute-start(bf16[2,128,768]{2,1,0:T(8,128)(2,1)} %get-tuple-element.51), channel_id=1, source_target_pairs={{0,2},{1,3},{2,0},{3,1},{4,6},{5,7},{6,4},{7,5},{8,10},{9,11},{10,... | collective-permute-start | bytes 1179656 | tf_op jit(solution)/shard_map/ppermute | solution.py:125
  92.1 12.2 %collective-permute-start.1 = (bf16[2,128,768]{2,1,0:T(8,128)(2,1)}, bf16[2,128,768]{2,1,0:T(8,128)(2,1)S(1)}, u32[]{:S(2)}, u32[]{:S(2)}) collective-permute-start(bf16[2,128,768]{2,1,0:T(8,128)(2,1)} %get-tuple-element.52), channel_id=1, source_target_pairs={{0,4},{1,5},{2,6},{3,7},{4,0},{5,1},{6,2},{7,3},{8,12},{9,13},{10,... | collective-permute-start | bytes 1179656 | tf_op jit(solution)/shard_map/ppermute | solution.py:125
  93.5 15.0 %collective-permute-start.2 = (bf16[2,128,768]{2,1,0:T(8,128)(2,1)}, bf16[2,128,768]{2,1,0:T(8,128)(2,1)S(1)}, u32[]{:S(2)}, u32[]{:S(2)}) collective-permute-start(bf16[2,128,768]{2,1,0:T(8,128)(2,1)} %get-tuple-element.53), channel_id=1, source_target_pairs={{0,6},{1,7},{2,4},{3,5},{4,2},{5,3},{6,0},{7,1},{8,14},{9,15},{10,... | collective-permute-start | bytes 1179656 | tf_op jit(solution)/shard_map/ppermute | solution.py:125
  98.6 11.3 %collective-permute-start.9 = (bf16[96,2432]{1,0:T(8,128)(2,1)}, bf16[96,2432]{1,0:T(8,128)(2,1)S(1)}, u32[]{:S(2)}, u32[]{:S(2)}) collective-permute-start(bf16[96,2432]{1,0:T(8,128)(2,1)} %join_qkv.1.refs_4_.refs_6_), channel_id=1, source_target_pairs={{0,1},{1,0},{2,3},{3,2},{4,5},{5,4},{6,7},{7,6},{8,9},{9,8},{10,11... | collective-permute-start | bytes 1400840 | tf_op jit(solution)/shard_map/ppermute | solution.py:116
  104.3 5.6 %collective-permute-start.10 = (bf16[96,2432]{1,0:T(8,128)(2,1)S(1)}, bf16[96,2432]{1,0:T(8,128)(2,1)S(1)}, u32[]{:S(2)}, u32[]{:S(2)}) collective-permute-start(bf16[96,2432]{1,0:T(8,128)(2,1)S(1)} %collective-permute-done.6.refs_5_.refs_7_), channel_id=1, source_target_pairs={{0,1},{1,0},{2,3},{3,2},{4,5},{5,4},{6,7},{7,6},{8,9},{9,8},{10,11... | collective-permute-start | bytes 1400840 | tf_op jit(solution)/shard_map/ppermute | solution.py:116
  104.4 5.6 %collective-permute-start.11 = (bf16[96,2432]{1,0:T(8,128)(2,1)S(1)}, bf16[96,2432]{1,0:T(8,128)(2,1)S(1)}, u32[]{:S(2)}, u32[]{:S(2)}) collective-permute-start(bf16[96,2432]{1,0:T(8,128)(2,1)S(1)} %collective-permute-done.7.refs_6_.refs_8_), channel_id=1, source_target_pairs={{0,1},{1,0},{2,3},{3,2},{4,5},{5,4},{6,7},{7,6},{8,9},{9,8},{10,11... | collective-permute-start | bytes 1400840 | tf_op jit(solution)/shard_map/ppermute | solution.py:116
  104.9 5.1 %collective-permute-start.12 = (bf16[96,2432]{1,0:T(8,128)(2,1)S(1)}, bf16[96,2432]{1,0:T(8,128)(2,1)S(1)}, u32[]{:S(2)}, u32[]{:S(2)}) collective-permute-start(bf16[96,2432]{1,0:T(8,128)(2,1)S(1)} %collective-permute-done.8.refs_7_.refs_9_), channel_id=1, source_target_pairs={{0,1},{1,0},{2,3},{3,2},{4,5},{5,4},{6,7},{7,6},{8,9},{9,8},{10,11... | collective-permute-start | bytes 1400840 | tf_op jit(solution)/shard_map/ppermute | solution.py:116
  108.5 12.5 %collective-permute-start.17 = (bf16[528,768]{1,0:T(8,128)(2,1)}, bf16[528,768]{1,0:T(8,128)(2,1)S(1)}, u32[]{:S(2)}, u32[]{:S(2)}) collective-permute-start(bf16[528,768]{1,0:T(8,128)(2,1)} %join_rest.1.refs_4_), channel_id=1, source_target_pairs={{0,2},{1,5},{2,0},{3,7},{4,6},{5,1},{6,4},{7,3},{8,10},{9,13},{10,... | collective-permute-start | bytes 2433032 | tf_op jit(solution)/shard_map/ppermute | solution.py:134
  118.5 22.4 %collective-permute-start.13 = (bf16[2,512,768]{2,1,0:T(8,128)(2,1)}, bf16[2,512,768]{2,1,0:T(8,128)(2,1)S(1)}, u32[]{:S(2)}, u32[]{:S(2)}) collective-permute-start(bf16[2,512,768]{2,1,0:T(8,128)(2,1)} %get-tuple-element.55.refs_0_), channel_id=1, source_target_pairs={{0,1},{1,0},{2,3},{3,2},{4,5},{5,4},{6,7},{7,6},{8,9},{9,8},{10,11... | collective-permute-start | bytes 4718600 | tf_op jit(solution)/shard_map/ppermute | solution.py:1045
  119.9 12.3 %collective-permute-start.18 = (bf16[528,768]{1,0:T(8,128)(2,1)S(1)}, bf16[528,768]{1,0:T(8,128)(2,1)S(1)}, u32[]{:S(2)}, u32[]{:S(2)}) collective-permute-start(bf16[528,768]{1,0:T(8,128)(2,1)S(1)} %copy-done.4), channel_id=1, source_target_pairs={{0,4},{1,3},{2,6},{3,1},{4,0},{5,7},{6,2},{7,5},{8,12},{9,11},{10,... | collective-permute-start | bytes 2433032 | tf_op jit(solution)/shard_map/ppermute | solution.py:134
  121.1 37.3 %copy-start.25 = (bf16[528,768]{1,0:T(8,128)(2,1)}, bf16[528,768]{1,0:T(8,128)(2,1)S(1)}, u32[]{:S(2)}) copy-start(bf16[528,768]{1,0:T(8,128)(2,1)S(1)} %collective-permute-done.17.refs_5_) | copy-start | bytes 2433028
  121.1 19.7 %collective-permute-start.19 = (bf16[528,768]{1,0:T(8,128)(2,1)S(1)}, bf16[528,768]{1,0:T(8,128)(2,1)S(1)}, u32[]{:S(2)}, u32[]{:S(2)}) collective-permute-start(bf16[528,768]{1,0:T(8,128)(2,1)S(1)} %collective-permute-done.17.refs_5_), channel_id=1, source_target_pairs={{0,4},{1,3},{2,6},{3,1},{4,0},{5,7},{6,2},{7,5},{8,12},{9,11},{10,... | collective-permute-start | bytes 2433032 | tf_op jit(solution)/shard_map/ppermute | solution.py:134
  122.3 36.2 %collective-permute-start.20 = (bf16[528,768]{1,0:T(8,128)(2,1)S(1)}, bf16[528,768]{1,0:T(8,128)(2,1)S(1)}, u32[]{:S(2)}, u32[]{:S(2)}) collective-permute-start(bf16[528,768]{1,0:T(8,128)(2,1)S(1)} %copy-done.4), channel_id=1, source_target_pairs={{0,1},{1,0},{2,3},{3,2},{4,5},{5,4},{6,7},{7,6},{8,9},{9,8},{10,11... | collective-permute-start | bytes 2433032 | tf_op jit(solution)/shard_map/ppermute | solution.py:116
  122.3 36.2 %collective-permute-start.21 = (bf16[528,768]{1,0:T(8,128)(2,1)S(1)}, bf16[528,768]{1,0:T(8,128)(2,1)S(1)}, u32[]{:S(2)}, u32[]{:S(2)}) collective-permute-start(bf16[528,768]{1,0:T(8,128)(2,1)S(1)} %collective-permute-done.17.refs_5_), channel_id=1, source_target_pairs={{0,1},{1,0},{2,3},{3,2},{4,5},{5,4},{6,7},{7,6},{8,9},{9,8},{10,11... | collective-permute-start | bytes 2433032 | tf_op jit(solution)/shard_map/ppermute | solution.py:116
  132.1 26.3 %collective-permute-start.22 = (bf16[528,768]{1,0:T(8,128)(2,1)S(1)}, bf16[528,768]{1,0:T(8,128)(2,1)S(1)}, u32[]{:S(2)}, u32[]{:S(2)}) collective-permute-start(bf16[528,768]{1,0:T(8,128)(2,1)S(1)} %collective-permute-done.18.refs_6_), channel_id=1, source_target_pairs={{0,1},{1,0},{2,3},{3,2},{4,5},{5,4},{6,7},{7,6},{8,9},{9,8},{10,11... | collective-permute-start | bytes 2433032 | tf_op jit(solution)/shard_map/ppermute | solution.py:116
  140.8 17.7 %collective-permute-start.23 = (bf16[528,768]{1,0:T(8,128)(2,1)S(1)}, bf16[528,768]{1,0:T(8,128)(2,1)S(1)}, u32[]{:S(2)}, u32[]{:S(2)}) collective-permute-start(bf16[528,768]{1,0:T(8,128)(2,1)S(1)} %collective-permute-done.19.refs_7_), channel_id=1, source_target_pairs={{0,1},{1,0},{2,3},{3,2},{4,5},{5,4},{6,7},{7,6},{8,9},{9,8},{10,11... | collective-permute-start | bytes 2433032 | tf_op jit(solution)/shard_map/ppermute | solution.py:116
  203.0 3.8 %collective-permute-start.27 = (bf16[2,512,768]{2,1,0:T(8,128)(2,1)}, bf16[2,512,768]{2,1,0:T(8,128)(2,1)S(1)}, u32[]{:S(2)}, u32[]{:S(2)}) collective-permute-start(bf16[2,512,768]{2,1,0:T(8,128)(2,1)} %get-tuple-element.70), channel_id=1, source_target_pairs={{0,1},{1,0},{2,3},{3,2},{4,5},{5,4},{6,7},{7,6},{8,9},{9,8},{10,11... | collective-permute-start | bytes 4718600 | tf_op jit(solution)/shard_map/ppermute | solution.py:1066
  222.4 2.6 collective-permute-start.31
  222.8 3.5 collective-permute-start.32
  223.3 5.3 %collective-permute-start.38 = (bf16[2,528,768]{2,1,0:T(8,128)(2,1)S(1)}, bf16[2,528,768]{2,1,0:T(8,128)(2,1)S(1)}, u32[]{:S(2)}, u32[]{:S(2)}) collective-permute-start(bf16[2,528,768]{2,1,0:T(8,128)(2,1)S(1)} %get-tuple-element.94), channel_id=1, source_target_pairs={{0,1},{1,0},{2,3},{3,2},{4,5},{5,4},{6,7},{7,6},{8,9},{9,8},{10,11... | collective-permute-start | bytes 4866056 | tf_op jit(solution)/shard_map/ppermute | solution.py:116
  223.8 7.2 %collective-permute-start.39 = (bf16[2,528,768]{2,1,0:T(8,128)(2,1)S(1)}, bf16[2,528,768]{2,1,0:T(8,128)(2,1)S(1)}, u32[]{:S(2)}, u32[]{:S(2)}) collective-permute-start(bf16[2,528,768]{2,1,0:T(8,128)(2,1)S(1)} %get-tuple-element.95), channel_id=1, source_target_pairs={{0,1},{1,0},{2,3},{3,2},{4,5},{5,4},{6,7},{7,6},{8,9},{9,8},{10,11... | collective-permute-start | bytes 4866056 | tf_op jit(solution)/shard_map/ppermute | solution.py:116
  226.7 13.6 %collective-permute-start.33 = (bf16[2,96,2432]{2,1,0:T(8,128)(2,1)S(1)}, bf16[2,96,2432]{2,1,0:T(8,128)(2,1)S(1)}, u32[]{:S(2)}, u32[]{:S(2)}) collective-permute-start(bf16[2,96,2432]{2,1,0:T(8,128)(2,1)S(1)} %get-tuple-element.97), channel_id=1, source_target_pairs={{0,4},{1,3},{2,6},{3,1},{4,0},{5,7},{6,2},{7,5},{8,12},{9,11},{10,... | collective-permute-start | bytes 2801672 | tf_op jit(solution)/shard_map/ppermute | solution.py:151
  231.7 35.3 %collective-permute-start.40 = (bf16[2,528,768]{2,1,0:T(8,128)(2,1)S(1)}, bf16[2,528,768]{2,1,0:T(8,128)(2,1)S(1)}, u32[]{:S(2)}, u32[]{:S(2)}) collective-permute-start(bf16[2,528,768]{2,1,0:T(8,128)(2,1)S(1)} %get-tuple-element.93), channel_id=1, source_target_pairs={{0,4},{1,3},{2,6},{3,1},{4,0},{5,7},{6,2},{7,5},{8,12},{9,11},{10,... | collective-permute-start | bytes 4866056 | tf_op jit(solution)/shard_map/ppermute | solution.py:151
  240.5 32.1 %collective-permute-start.34 = (bf16[1,96,2432]{2,1,0:T(8,128)(2,1)S(1)}, bf16[1,96,2432]{2,1,0:T(8,128)(2,1)S(1)}, u32[]{:S(2)}, u32[]{:S(2)}) collective-permute-start(bf16[1,96,2432]{2,1,0:T(8,128)(2,1)S(1)} %add_convert_fusion.8), channel_id=1, source_target_pairs={{0,2},{1,5},{2,0},{3,7},{4,6},{5,1},{6,4},{7,3},{8,10},{9,13},{10,... | collective-permute-start | bytes 1400840 | tf_op jit(solution)/shard_map/ppermute | solution.py:151
  241.3 26.6 %collective-permute-start.24 = (bf16[128,768]{1,0:T(8,128)(2,1)S(1)}, bf16[128,768]{1,0:T(8,128)(2,1)S(1)}, u32[]{:S(2)}, u32[]{:S(2)}) collective-permute-start(bf16[128,768]{1,0:T(8,128)(2,1)S(1)} %copy-done.47), channel_id=1, source_target_pairs={{0,2},{1,3},{2,0},{3,1},{4,6},{5,7},{6,4},{7,5},{8,10},{9,11},{10,... | collective-permute-start | bytes 589832 | tf_op jit(solution)/shard_map/ppermute | solution.py:125
  242.6 28.6 %collective-permute-start.25 = (bf16[128,768]{1,0:T(8,128)(2,1)S(1)}, bf16[128,768]{1,0:T(8,128)(2,1)S(1)}, u32[]{:S(2)}, u32[]{:S(2)}) collective-permute-start(bf16[128,768]{1,0:T(8,128)(2,1)S(1)} %copy-done.45), channel_id=1, source_target_pairs={{0,4},{1,5},{2,6},{3,7},{4,0},{5,1},{6,2},{7,3},{8,12},{9,13},{10,... | collective-permute-start | bytes 589832 | tf_op jit(solution)/shard_map/ppermute | solution.py:125
  243.4 32.2 %collective-permute-start.26 = (bf16[128,768]{1,0:T(8,128)(2,1)S(1)}, bf16[128,768]{1,0:T(8,128)(2,1)S(1)}, u32[]{:S(2)}, u32[]{:S(2)}) collective-permute-start(bf16[128,768]{1,0:T(8,128)(2,1)S(1)} %copy-done.42), channel_id=1, source_target_pairs={{0,6},{1,7},{2,4},{3,5},{4,2},{5,3},{6,0},{7,1},{8,14},{9,15},{10,... | collective-permute-start | bytes 589832 | tf_op jit(solution)/shard_map/ppermute | solution.py:125
  267.0 16.3 %collective-permute-start.28 = (bf16[128,768]{1,0:T(8,128)(2,1)S(1)}, bf16[128,768]{1,0:T(8,128)(2,1)S(1)}, u32[]{:S(2)}, u32[]{:S(2)}) collective-permute-start(bf16[128,768]{1,0:T(8,128)(2,1)S(1)} %copy-done.46), channel_id=1, source_target_pairs={{0,2},{1,3},{2,0},{3,1},{4,6},{5,7},{6,4},{7,5},{8,10},{9,11},{10,... | collective-permute-start | bytes 589832 | tf_op jit(solution)/shard_map/ppermute | solution.py:125
  268.0 18.0 %collective-permute-start.29 = (bf16[128,768]{1,0:T(8,128)(2,1)S(1)}, bf16[128,768]{1,0:T(8,128)(2,1)S(1)}, u32[]{:S(2)}, u32[]{:S(2)}) collective-permute-start(bf16[128,768]{1,0:T(8,128)(2,1)S(1)} %copy-done.44), channel_id=1, source_target_pairs={{0,4},{1,5},{2,6},{3,7},{4,0},{5,1},{6,2},{7,3},{8,12},{9,13},{10,... | collective-permute-start | bytes 589832 | tf_op jit(solution)/shard_map/ppermute | solution.py:125
  271.2 41.9 %collective-permute-start.30 = (bf16[128,768]{1,0:T(8,128)(2,1)S(1)}, bf16[128,768]{1,0:T(8,128)(2,1)S(1)}, u32[]{:S(2)}, u32[]{:S(2)}) collective-permute-start(bf16[128,768]{1,0:T(8,128)(2,1)S(1)} %copy-done.43), channel_id=1, source_target_pairs={{0,6},{1,7},{2,4},{3,5},{4,2},{5,3},{6,0},{7,1},{8,14},{9,15},{10,... | collective-permute-start | bytes 589832 | tf_op jit(solution)/shard_map/ppermute | solution.py:125
  272.6 69.4 %collective-permute-start.41 = (bf16[1,528,768]{2,1,0:T(8,128)(2,1)S(1)}, bf16[1,528,768]{2,1,0:T(8,128)(2,1)S(1)}, u32[]{:S(2)}, u32[]{:S(2)}) collective-permute-start(bf16[1,528,768]{2,1,0:T(8,128)(2,1)S(1)} %add_convert_fusion.5), channel_id=1, source_target_pairs={{0,2},{1,5},{2,0},{3,7},{4,6},{5,1},{6,4},{7,3},{8,10},{9,13},{10,... | collective-permute-start | bytes 2433032 | tf_op jit(solution)/shard_map/ppermute | solution.py:151
  275.6 63.8 %collective-permute-start.35 = (bf16[96,640]{1,0:T(8,128)(2,1)}, bf16[96,640]{1,0:T(8,128)(2,1)S(1)}, u32[]{:S(2)}, u32[]{:S(2)}) collective-permute-start(bf16[96,640]{1,0:T(8,128)(2,1)} %get-tuple-element.78), channel_id=1, source_target_pairs={{0,8},{8,0},{16,24},{24,16},{1,9},{9,1},{17,25},{25,17},{2,10},{10... | collective-permute-start | bytes 368648 | tf_op jit(solution)/shard_map/ppermute | solution.py:937
  283.2 56.2 %collective-permute-start.36 = (bf16[96,640]{1,0:T(8,128)(2,1)}, bf16[96,640]{1,0:T(8,128)(2,1)S(1)}, u32[]{:S(2)}, u32[]{:S(2)}) collective-permute-start(bf16[96,640]{1,0:T(8,128)(2,1)} %get-tuple-element.79), channel_id=1, source_target_pairs={{0,16},{8,24},{16,0},{24,8},{1,17},{9,25},{17,1},{25,9},{2,18},{10... | collective-permute-start | bytes 368648 | tf_op jit(solution)/shard_map/ppermute | solution.py:937
  286.0 53.5 %collective-permute-start.37 = (bf16[96,640]{1,0:T(8,128)(2,1)}, bf16[96,640]{1,0:T(8,128)(2,1)S(1)}, u32[]{:S(2)}, u32[]{:S(2)}) collective-permute-start(bf16[96,640]{1,0:T(8,128)(2,1)} %get-tuple-element.80), channel_id=1, source_target_pairs={{0,24},{8,16},{16,8},{24,0},{1,25},{9,17},{17,9},{25,1},{2,26},{10... | collective-permute-start | bytes 368648 | tf_op jit(solution)/shard_map/ppermute | solution.py:937
  345.5 8.9 %collective-permute-start.42 = (bf16[288,384]{1,0:T(8,128)(2,1)}, bf16[288,384]{1,0:T(8,128)(2,1)S(1)}, u32[]{:S(2)}, u32[]{:S(2)}) collective-permute-start(bf16[288,384]{1,0:T(8,128)(2,1)} %get-tuple-element.86), channel_id=1, source_target_pairs={{0,8},{8,0},{16,24},{24,16},{1,9},{9,1},{17,25},{25,17},{2,10},{10... | collective-permute-start | bytes 663560 | tf_op jit(solution)/shard_map/ppermute | solution.py:937
  348.1 17.4 %collective-permute-start.43 = (bf16[288,384]{1,0:T(8,128)(2,1)}, bf16[288,384]{1,0:T(8,128)(2,1)S(1)}, u32[]{:S(2)}, u32[]{:S(2)}) collective-permute-start(bf16[288,384]{1,0:T(8,128)(2,1)} %get-tuple-element.87), channel_id=1, source_target_pairs={{0,16},{8,24},{16,0},{24,8},{1,17},{9,25},{17,1},{25,9},{2,18},{10... | collective-permute-start | bytes 663560 | tf_op jit(solution)/shard_map/ppermute | solution.py:937
  348.5 17.0 %collective-permute-start.44 = (bf16[288,384]{1,0:T(8,128)(2,1)}, bf16[288,384]{1,0:T(8,128)(2,1)S(1)}, u32[]{:S(2)}, u32[]{:S(2)}) collective-permute-start(bf16[288,384]{1,0:T(8,128)(2,1)} %get-tuple-element.88), channel_id=1, source_target_pairs={{0,24},{8,16},{16,8},{24,0},{1,25},{9,17},{17,9},{25,1},{2,26},{10... | collective-permute-start | bytes 663560 | tf_op jit(solution)/shard_map/ppermute | solution.py:937
  (45 other events, 395.5 us)
